TPU v7x, 32 devices: a whole 2x2x4 slice. The times are simulated.
32 devices in a mesh: groups: 2 (over y), gx: 4 (over z), gy: 2 (over x), gz: 2 (over core).
Axes of the slice: x: 2, y: 2, z: 4, core: 2. Of those that a mesh axis runs over, the one named last changes fastest.
Arguments:
- parent: bfloat16 [160, 32, 1024], P('groups', 'gx', ('gy', 'gz')), parts along dimension 0, may hold values from -6 to 6
- nest: bfloat16 [160, 24, 1536], P('groups', 'gx', ('gy', 'gz')), parts along dimension 0, may hold values from -6 to 6
- nu_parent: float32 [80], replicated, may hold values from 0.03 to 0.24
- nu_nest: float32 [80], replicated, may hold values from 0.03 to 0.24
- relax: float32 [80], replicated, may hold values from 0.1 to 0.5
- feedback: float32 [80], replicated, may hold values from 0.3 to 1
- vert_mix: float32 [80, 80], replicated, may hold values from -1 to 1
- fp_owner: int32 [4, 4, 256, 1], P('gx', ('gy', 'gz')), may hold values from 0 to 3; in each aligned block of 256 rows (0 to 255, 256 to 511, ..., all dimensions but the last counted through in order) at most 256 rows name the same one
- fp_cell: int32 [4, 4, 256], P('gx', ('gy', 'gz')), may hold values from 0 to 2047
- nest_of: int32 [24], replicated, may hold values from 0 to 2, as said below
Outputs:
- parent_out: bfloat16 [160, 32, 1024], P('groups', 'gx', ('gy', 'gz')), parts along dimension 0
- nest_out: bfloat16 [160, 24, 1536], P('groups', 'gx', ('gy', 'gz')), parts along dimension 0
There are 2 independent parts, one for each index of `groups`. A program takes and returns all parts, laid end to end along the dimension named above; an argument that names none is the same for every part. Nothing has to cross between parts.
Inputs may be any that keep to these rules, and one draw needn't show every extreme that they name: `fp_owner`: within the 256 blocks of one nest tile no parent tile is named more than 256 times; in some nest tiles one is named exactly 256 times. `nest_of`: never falls along the rows; every nest holds one or more rows; nest 1 holds rows 11 and 12.
All inputs are finite; a program needn't handle non-finite values.
Results may differ from a plain program's by a relative error of at most 0.0033.
Values may be sent and summed in bfloat16 or wider, within the bound.
A program may use at most 64 MiB of HBM per device.

v0:
```python
import jax
import jax.numpy as jnp
from jax import lax
from jax.sharding import PartitionSpec as P


def extended(block, sides, width):
    for axis, dim in sides:
        count = lax.axis_size(axis)
        forward = [(i, i + 1) for i in range(count - 1)]
        backward = [(target, source) for source, target in forward]
        low = lax.ppermute(
            lax.slice_in_dim(block, block.shape[dim] - width, None, axis=dim), axis, forward
        )
        high = lax.ppermute(lax.slice_in_dim(block, 0, width, axis=dim), axis, backward)
        block = jnp.concatenate([low, block, high], axis=dim)
    return block


def mix_levels(matrix, values):
    flat_values = values.reshape(values.shape[0], -1)
    mixed = jnp.dot(
        matrix, flat_values, precision=lax.Precision.HIGHEST, preferred_element_type=jnp.float32
    )
    return mixed.reshape(values.shape)


def stencil(padded, centre):
    return (
        padded[:, 2:, 1:-1]
        + padded[:, :-2, 1:-1]
        + padded[:, 1:-1, 2:]
        + padded[:, 1:-1, :-2]
        - 4.0 * centre
    )


def nest_stencil(padded, centre, left_w, right_w):
    return (
        padded[:, 2:, 1:-1] * right_w[None, :, None]
        + padded[:, :-2, 1:-1] * left_w[None, :, None]
        + padded[:, 1:-1, 2:]
        + padded[:, 1:-1, :-2]
        - 4.0 * centre
    )


def advance(padded, centre, target, nu_nest, relax, vert_mix, left_w, right_w):
    moved = centre + nu_nest[:, None, None] * nest_stencil(padded, centre, left_w, right_w)
    moved = moved + relax[:, None, None] * (target - moved)
    return mix_levels(vert_mix, moved)


def nest_segments(nest_of, first, count):
    index_rows = first + jnp.arange(count, dtype=jnp.int32)
    inside = (index_rows >= 0) & (index_rows < nest_of.shape[0])
    return jnp.where(inside, nest_of[jnp.clip(index_rows, 0, nest_of.shape[0] - 1)], -1)


def row_weights(segments):
    left_w = (segments[:-2] == segments[1:-1]).astype(jnp.float32)
    right_w = (segments[2:] == segments[1:-1]).astype(jnp.float32)
    return (left_w, right_w)


def body(parent, nest, nu_parent, nu_nest, relax, feedback, vert_mix, fp_owner, fp_cell, nest_of):
    levels = parent.shape[0]
    tiles_x = lax.axis_size("gx")
    here_x = lax.axis_index("gx")
    coarse_rim = extended(parent, (("gx", 1), (("gy", "gz"), 2)), 1).astype(jnp.float32)
    centre = coarse_rim[:, 1:-1, 1:-1]
    stepped = mix_levels(vert_mix, centre + nu_parent[:, None, None] * stencil(coarse_rim, centre))
    flat_parent = stepped.reshape(levels, -1)
    owners = fp_owner.reshape(-1)
    cells = fp_cell.reshape(-1)
    requests = owners.shape[0]
    slots = 4 * requests // tiles_x
    onehot = (owners[:, None] == jnp.arange(tiles_x, dtype=jnp.int32)[None, :]).astype(jnp.int32)
    before = jnp.cumsum(onehot, axis=0) - onehot
    order_in = jnp.sum(before * onehot, axis=1)
    places = owners * slots + order_in
    wanted = jnp.zeros((tiles_x * slots,), jnp.int32).at[places].set(cells)
    served_ids = lax.all_to_all(wanted, "gx", split_axis=0, concat_axis=0, tiled=True)
    answers = lax.all_to_all(
        jnp.take(flat_parent, served_ids, axis=1), "gx", split_axis=1, concat_axis=1, tiled=True
    )
    forcing_flat = jnp.take(answers, places, axis=1)
    nest_rows = nest.shape[1]
    nest_cols = nest.shape[2]
    block_rows = nest_rows // 3
    block_cols = nest_cols // 3
    forcing_block = forcing_flat.reshape(levels, block_rows, block_cols)
    row_start = here_x * nest_rows
    forcing_full = jnp.repeat(jnp.repeat(forcing_block, 3, axis=1), 3, axis=2)
    left_w, right_w = row_weights(nest_segments(nest_of, row_start - 1, nest_rows + 2))
    nest_state = nest.astype(jnp.float32)
    for turn_no in range(3):
        padded = extended(
            nest_state.astype(jnp.bfloat16), (("gx", 1), (("gy", "gz"), 2)), 1
        ).astype(nest_state.dtype)
        nest_state = advance(
            padded, nest_state, forcing_full, nu_nest, relax, vert_mix, left_w, right_w
        )
    blocks = nest_state.reshape(levels, block_rows, 3, block_cols, 3).mean(axis=(2, 4))
    nudge_gap = (blocks - forcing_block).reshape(levels, -1)
    outgoing = jnp.zeros((levels, tiles_x * slots), jnp.float32).at[:, places].set(nudge_gap)
    incoming = lax.all_to_all(outgoing, "gx", split_axis=1, concat_axis=1, tiled=True)
    summed = jnp.zeros_like(flat_parent).at[:, served_ids].add(incoming)
    parent_out = (stepped + feedback[:, None, None] * summed.reshape(stepped.shape)).astype(
        jnp.bfloat16
    )
    return (parent_out, nest_state.astype(jnp.bfloat16))


def solution(mesh):
    placed = (
        P("groups", "gx", ("gy", "gz")),
        P("groups", "gx", ("gy", "gz")),
        P(),
        P(),
        P(),
        P(),
        P(),
        P("gx", ("gy", "gz"), None, None),
        P("gx", ("gy", "gz"), None),
        P(),
    )
    return jax.shard_map(
        body,
        mesh=mesh,
        in_specs=placed,
        out_specs=(P("groups", "gx", ("gy", "gz")), P("groups", "gx", ("gy", "gz"))),
        check_vma=False,
    )
```

profile of v0, /device:TPU:1, one launch (start us, length us, event | category | flops | bytes accessed | tf_op | source)
XLA Modules:
  0.0 138.6 jit_solution(6008696607934461132)
XLA Ops:
  4.4 2.1 %scatter_custom_fusion = s32[1024]{0:T(1024)} fusion(s32[256]{0:T(256)S(1)} %bitcast.129, s32[256]{0:T(256)} %bitcast.133, s32[]{:T(128)} %constant.22.clone.1), kind=kCustom, calls=%fused_computation.87 | custom fusion | bytes 4608 | tf_op jit(solution)/shard_map/scatter | solution.py:82
  6.5 5.4 %all-to-all-start = ((s32[4,256,1]{1,2,0:T(1,128)}), s32[4,256,1]{1,2,0:T(1,128)S(1)}, u32[]{:S(2)}, u32[]{:S(2)}) async-start(s32[4,256,1]{1,2,0:T(1,128)} %bitcast.9), calls=%async_computation | async-start | bytes 8192 | tf_op jit(solution)/shard_map/all_to_all | solution.py:83
  13.2 3.4 %collective-permute-start = (bf16[80,1,256]{2,1,0:T(2,128)(2,1)S(1)}, bf16[80,1,256]{2,1,0:T(2,128)(2,1)S(1)}, u32[]{:S(2)}, u32[]{:S(2)}) collective-permute-start(bf16[80,1,256]{2,1,0:T(2,128)(2,1)S(1)} %get-tuple-element.24), channel_id=1, source_target_pairs={{0,4},{4,8},{8,12},{1,5},{5,9},{9,13},{2,6},{6,10},{10,14},{3,7},{... | collective-permute-start | bytes 122888 | tf_op jit(solution)/shard_map/ppermute | solution.py:12
  19.8 4.0 %collective-permute-start.4 = (bf16[80,1,384]{0,2,1:T(8,128)(2,1)}, bf16[80,1,384]{0,2,1:T(8,128)(2,1)S(1)}, u32[]{:S(2)}, u32[]{:S(2)}) collective-permute-start(bf16[80,1,384]{0,2,1:T(8,128)(2,1)} %get-tuple-element.22), channel_id=1, source_target_pairs={{0,4},{4,8},{8,12},{1,5},{5,9},{9,13},{2,6},{6,10},{10,14},{3,7},{... | collective-permute-start | bytes 184328 | tf_op jit(solution)/shard_map/ppermute | solution.py:12
  27.0 5.1 %collective-permute-start.2 = (bf16[80,10,1]{2,1,0:T(8,128)(2,1)S(1)}, bf16[80,10,1]{2,1,0:T(8,128)(2,1)S(1)}, u32[]{:S(2)}, u32[]{:S(2)}) collective-permute-start(bf16[80,10,1]{2,1,0:T(8,128)(2,1)S(1)} %get-tuple-element.16), channel_id=1, source_target_pairs={{0,1},{1,2},{2,3},{4,5},{5,6},{6,7},{8,9},{9,10},{10,11},{12,13},{... | collective-permute-start | bytes 4808 | tf_op jit(solution)/shard_map/ppermute | solution.py:12
  32.1 1.9 %collective-permute-start.3 = (bf16[80,10,1]{2,1,0:T(8,128)(2,1)S(1)}, bf16[80,10,1]{2,1,0:T(8,128)(2,1)S(1)}, u32[]{:S(2)}, u32[]{:S(2)}) collective-permute-start(bf16[80,10,1]{2,1,0:T(8,128)(2,1)S(1)} %get-tuple-element.17), channel_id=1, source_target_pairs={{1,0},{2,1},{3,2},{5,4},{6,5},{7,6},{9,8},{10,9},{11,10},{13,12},{... | collective-permute-start | bytes 4808 | tf_op jit(solution)/shard_map/ppermute | solution.py:15
  34.1 2.0 %collective-permute-done.2 = bf16[80,10,1]{2,1,0:T(8,128)(2,1)S(1)} collective-permute-done((bf16[80,10,1]{2,1,0:T(8,128)(2,1)S(1)}, bf16[80,10,1]{2,1,0:T(8,128)(2,1)S(1)}, u32[]{:S(2)}, u32[]{:S(2)}) %collective-permute-start.2) | collective-permute-done | bytes 1632 | tf_op jit(solution)/shard_map/ppermute | solution.py:12
  36.1 4.4 %collective-permute-done.3 = bf16[80,10,1]{2,1,0:T(8,128)(2,1)S(1)} collective-permute-done((bf16[80,10,1]{2,1,0:T(8,128)(2,1)S(1)}, bf16[80,10,1]{2,1,0:T(8,128)(2,1)S(1)}, u32[]{:S(2)}, u32[]{:S(2)}) %collective-permute-start.3) | collective-permute-done | bytes 1632 | tf_op jit(solution)/shard_map/ppermute | solution.py:15
  43.8 2.8 %gather_fusion.1 = f32[1024,80]{1,0:T(8,128)S(1)} fusion(f32[80,2048]{0,1:T(8,128)S(1)} %copy.71, s32[1024]{0:T(1024)S(1)} %broadcast_clamp_fusion), kind=kCustom, calls=%fused_computation.1 | custom fusion | bytes 659456 | tf_op jit(solution)/shard_map/jit(_take)/gather | solution.py:85
  47.6 5.4 %all-to-all-start.1 = ((f32[80,4,256]{2,0,1:T(8,128)}), f32[80,4,256]{2,0,1:T(8,128)S(1)}, u32[]{:S(2)}, u32[]{:S(2)}) async-start(f32[80,4,256]{2,0,1:T(8,128)} %broadcast_select_fusion), calls=%async_computation.1 | async-start | bytes 655360 | tf_op jit(solution)/shard_map/all_to_all | solution.py:84
  53.7 2.0 %collective-permute-start.6 = (bf16[80,8,1]{0,2,1:T(2,128)(2,1)S(1)}, bf16[80,8,1]{0,2,1:T(2,128)(2,1)S(1)}, u32[]{:S(2)}, u32[]{:S(2)}) collective-permute-start(bf16[80,8,1]{0,2,1:T(2,128)(2,1)S(1)} %get-tuple-element.14), channel_id=1, source_target_pairs={{0,1},{1,2},{2,3},{4,5},{5,6},{6,7},{8,9},{9,10},{10,11},{12,13},{... | collective-permute-start | bytes 3848 | tf_op jit(solution)/shard_map/ppermute | solution.py:12
  55.7 2.3 %collective-permute-start.7 = (bf16[80,8,1]{0,2,1:T(2,128)(2,1)S(1)}, bf16[80,8,1]{0,2,1:T(2,128)(2,1)S(1)}, u32[]{:S(2)}, u32[]{:S(2)}) collective-permute-start(bf16[80,8,1]{0,2,1:T(2,128)(2,1)S(1)} %get-tuple-element.15), channel_id=1, source_target_pairs={{1,0},{2,1},{3,2},{5,4},{6,5},{7,6},{9,8},{10,9},{11,10},{13,12},{... | collective-permute-start | bytes 3848 | tf_op jit(solution)/shard_map/ppermute | solution.py:15
  58.1 2.6 %collective-permute-done.7 = bf16[80,8,1]{0,2,1:T(2,128)(2,1)S(1)} collective-permute-done((bf16[80,8,1]{0,2,1:T(2,128)(2,1)S(1)}, bf16[80,8,1]{0,2,1:T(2,128)(2,1)S(1)}, u32[]{:S(2)}, u32[]{:S(2)}) %collective-permute-start.7) | collective-permute-done | bytes 1312 | tf_op jit(solution)/shard_map/ppermute | solution.py:15
  64.4 2.2 %reshape.183 = f32[80,6,384]{0,2,1:T(8,128)S(1)} reshape(f32[80,6,128,3]{0,3,2,1:T(4,128)} %broadcast_in_dim.67) | data formatting | bytes 1474560 | tf_op jit(solution)/shard_map/reshape | solution.py:94
  68.0 2.3 %convolution_bitcast_fusion.2 = f32[80,2304]{1,0:T(8,128)} fusion(f32[80,2304]{0,1:T(8,128)S(1)} %bitcast.108, f32[80,80]{1,0:T(8,128)S(1)} %copy-done), kind=kOutput, calls=%fused_computation.8 | convolution fusion | flops 176947200 | bytes 1500160 | tf_op jit(solution)/shard_map/dot_general | solution.py:22
  70.3 1.5 %copy.92 = f32[80,2304]{0,1:T(8,128)S(1)} copy(f32[80,2304]{1,0:T(8,128)} %convolution_bitcast_fusion.2) | data formatting | bytes 1474560 | tf_op jit(solution)/shard_map/reshape | solution.py:25
  71.9 3.7 %collective-permute-start.8 = (bf16[80,1,384]{0,2,1:T(8,128)(2,1)S(1)}, bf16[80,1,384]{0,2,1:T(8,128)(2,1)S(1)}, u32[]{:S(2)}, u32[]{:S(2)}) collective-permute-start(bf16[80,1,384]{0,2,1:T(8,128)(2,1)S(1)} %get-tuple-element.20), channel_id=1, source_target_pairs={{0,4},{4,8},{8,12},{1,5},{5,9},{9,13},{2,6},{6,10},{10,14},{3,7},{... | collective-permute-start | bytes 184328 | tf_op jit(solution)/shard_map/ppermute | solution.py:12
  77.2 3.8 %collective-permute-done.9 = bf16[80,1,384]{0,2,1:T(8,128)(2,1)S(1)} collective-permute-done((bf16[80,1,384]{0,2,1:T(8,128)(2,1)S(1)}, bf16[80,1,384]{0,2,1:T(8,128)(2,1)S(1)}, u32[]{:S(2)}, u32[]{:S(2)}) %collective-permute-start.9) | collective-permute-done | bytes 61472 | tf_op jit(solution)/shard_map/ppermute | solution.py:15
  81.0 3.3 %collective-permute-start.10 = (bf16[80,8,1]{0,2,1:T(2,128)(2,1)S(1)}, bf16[80,8,1]{0,2,1:T(2,128)(2,1)S(1)}, u32[]{:S(2)}, u32[]{:S(2)}) collective-permute-start(bf16[80,8,1]{0,2,1:T(2,128)(2,1)S(1)} %get-tuple-element.12), channel_id=1, source_target_pairs={{0,1},{1,2},{2,3},{4,5},{5,6},{6,7},{8,9},{9,10},{10,11},{12,13},{... | collective-permute-start | bytes 3848 | tf_op jit(solution)/shard_map/ppermute | solution.py:12
  84.4 2.1 %collective-permute-start.11 = (bf16[80,8,1]{0,2,1:T(2,128)(2,1)S(1)}, bf16[80,8,1]{0,2,1:T(2,128)(2,1)S(1)}, u32[]{:S(2)}, u32[]{:S(2)}) collective-permute-start(bf16[80,8,1]{0,2,1:T(2,128)(2,1)S(1)} %get-tuple-element.13), channel_id=1, source_target_pairs={{1,0},{2,1},{3,2},{5,4},{6,5},{7,6},{9,8},{10,9},{11,10},{13,12},{... | collective-permute-start | bytes 3848 | tf_op jit(solution)/shard_map/ppermute | solution.py:15
  86.5 2.8 %collective-permute-done.11 = bf16[80,8,1]{0,2,1:T(2,128)(2,1)S(1)} collective-permute-done((bf16[80,8,1]{0,2,1:T(2,128)(2,1)S(1)}, bf16[80,8,1]{0,2,1:T(2,128)(2,1)S(1)}, u32[]{:S(2)}, u32[]{:S(2)}) %collective-permute-start.11) | collective-permute-done | bytes 1312 | tf_op jit(solution)/shard_map/ppermute | solution.py:15
  90.3 2.3 %convolution_bitcast_fusion.1 = f32[80,2304]{1,0:T(8,128)} fusion(f32[80,2304]{0,1:T(8,128)S(1)} %bitcast.107, f32[80,80]{1,0:T(8,128)S(1)} %copy-done), kind=kOutput, calls=%fused_computation.7 | convolution fusion | flops 176947200 | bytes 1500160 | tf_op jit(solution)/shard_map/dot_general | solution.py:22
  92.5 1.5 %copy.93 = f32[80,2304]{0,1:T(8,128)S(1)} copy(f32[80,2304]{1,0:T(8,128)} %convolution_bitcast_fusion.1) | data formatting | bytes 1474560 | tf_op jit(solution)/shard_map/reshape | solution.py:25
  94.1 3.1 %collective-permute-start.12 = (bf16[80,1,384]{0,2,1:T(8,128)(2,1)S(1)}, bf16[80,1,384]{0,2,1:T(8,128)(2,1)S(1)}, u32[]{:S(2)}, u32[]{:S(2)}) collective-permute-start(bf16[80,1,384]{0,2,1:T(8,128)(2,1)S(1)} %get-tuple-element.18), channel_id=1, source_target_pairs={{0,4},{4,8},{8,12},{1,5},{5,9},{9,13},{2,6},{6,10},{10,14},{3,7},{... | collective-permute-start | bytes 184328 | tf_op jit(solution)/shard_map/ppermute | solution.py:12
  98.9 3.7 %collective-permute-done.13 = bf16[80,1,384]{0,2,1:T(8,128)(2,1)S(1)} collective-permute-done((bf16[80,1,384]{0,2,1:T(8,128)(2,1)S(1)}, bf16[80,1,384]{0,2,1:T(8,128)(2,1)S(1)}, u32[]{:S(2)}, u32[]{:S(2)}) %collective-permute-start.13) | collective-permute-done | bytes 61472 | tf_op jit(solution)/shard_map/ppermute | solution.py:15
  102.6 3.4 %collective-permute-start.14 = (bf16[80,8,1]{0,2,1:T(2,128)(2,1)S(1)}, bf16[80,8,1]{0,2,1:T(2,128)(2,1)S(1)}, u32[]{:S(2)}, u32[]{:S(2)}) collective-permute-start(bf16[80,8,1]{0,2,1:T(2,128)(2,1)S(1)} %get-tuple-element.10), channel_id=1, source_target_pairs={{0,1},{1,2},{2,3},{4,5},{5,6},{6,7},{8,9},{9,10},{10,11},{12,13},{... | collective-permute-start | bytes 3848 | tf_op jit(solution)/shard_map/ppermute | solution.py:12
  106.0 1.9 %collective-permute-start.15 = (bf16[80,8,1]{0,2,1:T(2,128)(2,1)S(1)}, bf16[80,8,1]{0,2,1:T(2,128)(2,1)S(1)}, u32[]{:S(2)}, u32[]{:S(2)}) collective-permute-start(bf16[80,8,1]{0,2,1:T(2,128)(2,1)S(1)} %get-tuple-element.11), channel_id=1, source_target_pairs={{1,0},{2,1},{3,2},{5,4},{6,5},{7,6},{9,8},{10,9},{11,10},{13,12},{... | collective-permute-start | bytes 3848 | tf_op jit(solution)/shard_map/ppermute | solution.py:15
  108.0 3.0 %collective-permute-done.15 = bf16[80,8,1]{0,2,1:T(2,128)(2,1)S(1)} collective-permute-done((bf16[80,8,1]{0,2,1:T(2,128)(2,1)S(1)}, bf16[80,8,1]{0,2,1:T(2,128)(2,1)S(1)}, u32[]{:S(2)}, u32[]{:S(2)}) %collective-permute-start.15) | collective-permute-done | bytes 1312 | tf_op jit(solution)/shard_map/ppermute | solution.py:15
  114.9 1.6 %scatter_custom_fusion.1 = f32[80,1024]{0,1:T(8,128)S(1)} fusion(s32[256]{0:T(256)} %bitcast.131, f32[]{:T(128)} %constant.21.clone.1, f32[80,256]{0,1:T(8,128)S(1)} %bitcast_subtract_fusion), kind=kCustom, calls=%fused_computation.53 | custom fusion | bytes 410112 | tf_op jit(solution)/shard_map/scatter | solution.py:106
  117.4 3.5 %all-to-all-start.2 = ((f32[80,4,256]{2,0,1:T(8,128)}), f32[80,4,256]{2,0,1:T(8,128)S(1)}, u32[]{:S(2)}, u32[]{:S(2)}) async-start(f32[80,4,256]{2,0,1:T(8,128)} %copy.84), calls=%async_computation.2 | async-start | bytes 655360 | tf_op jit(solution)/shard_map/all_to_all | solution.py:107
  121.8 8.2 %all-to-all-done.2 = f32[80,4,256]{2,0,1:T(8,128)S(1)} async-done(((f32[80,4,256]{2,0,1:T(8,128)}), f32[80,4,256]{2,0,1:T(8,128)S(1)}, u32[]{:S(2)}, u32[]{:S(2)}) %all-to-all-start.2) | async-done | bytes 327712 | tf_op jit(solution)/shard_map/all_to_all | solution.py:107
  130.2 7.1 %scatter_custom_fusion.2 = f32[80,2048]{0,1:T(8,128)S(1)} fusion(s32[1024]{0:T(1024)S(1)} %bitcast.127, f32[1024,80]{1,0:T(8,128)S(1)} %copy.86, f32[]{:T(128)} %constant.21.clone.1), kind=kCustom, calls=%fused_computation.50 | custom fusion | flops 81920 | bytes 655364 | tf_op jit(solution)/shard_map/scatter-add | solution.py:108
  (113 shorter events, 33.0 us)
Async XLA Ops:
  0.6 42.1 %copy-start = (f32[80,80]{1,0:T(8,128)S(1)}, f32[80,80]{1,0:T(8,128)}, u32[]{:S(2)}) copy-start(f32[80,80]{1,0:T(8,128)} %param.16) | copy-start | bytes 76804
  0.6 24.5 %copy-start.6 = (s32[1,1,256,1]{2,3,1,0:T(1,128)S(1)}, s32[1,1,256,1]{2,3,1,0:T(1,128)}, u32[]{:S(2)}) copy-start(s32[1,1,256,1]{2,3,1,0:T(1,128)} %param.17) | copy-start | bytes 3076
  0.7 25.8 %copy-start.4 = (bf16[80,8,256]{2,1,0:T(8,128)(2,1)S(1)}, bf16[80,8,256]{2,1,0:T(8,128)(2,1)}, u32[]{:S(2)}) copy-start(bf16[80,8,256]{2,1,0:T(8,128)(2,1)} %param.10) | copy-start | bytes 983044
  0.7 25.0 %copy-start.1 = (s32[24]{0:T(128)S(1)}, s32[24]{0:T(128)}, u32[]{:S(2)}) copy-start(s32[24]{0:T(128)} %param.19) | copy-start | bytes 292
  3.7 22.7 %copy-start.7 = (s32[256]{0:T(256)}, s32[256]{0:T(256)S(1)}, u32[]{:S(2)}) copy-start(s32[256]{0:T(256)S(1)} %fusion.22) | copy-start | bytes 3076
  4.4 53.6 %copy-start.13 = (s32[256,1]{0,1:T(1,128)}, s32[256,1]{0,1:T(1,128)S(1)}, u32[]{:S(2)}) copy-start(s32[256,1]{0,1:T(1,128)S(1)} %compare_select_fusion.2) | copy-start | bytes 3076
  6.5 19.8 %all-to-all-start = ((s32[4,256,1]{1,2,0:T(1,128)}), s32[4,256,1]{1,2,0:T(1,128)S(1)}, u32[]{:S(2)}, u32[]{:S(2)}) async-start(s32[4,256,1]{1,2,0:T(1,128)} %bitcast.9), calls=%async_computation | async-start | bytes 8192 | tf_op jit(solution)/shard_map/all_to_all | solution.py:83
  13.2 13.2 %collective-permute-start = (bf16[80,1,256]{2,1,0:T(2,128)(2,1)S(1)}, bf16[80,1,256]{2,1,0:T(2,128)(2,1)S(1)}, u32[]{:S(2)}, u32[]{:S(2)}) collective-permute-start(bf16[80,1,256]{2,1,0:T(2,128)(2,1)S(1)} %get-tuple-element.24), channel_id=1, source_target_pairs={{0,4},{4,8},{8,12},{1,5},{5,9},{9,13},{2,6},{6,10},{10,14},{3,7},{... | collective-permute-start | bytes 122888 | tf_op jit(solution)/shard_map/ppermute | solution.py:12
  16.6 9.9 %collective-permute-start.1 = (bf16[80,1,256]{2,1,0:T(2,128)(2,1)S(1)}, bf16[80,1,256]{2,1,0:T(2,128)(2,1)S(1)}, u32[]{:S(2)}, u32[]{:S(2)}) collective-permute-start(bf16[80,1,256]{2,1,0:T(2,128)(2,1)S(1)} %get-tuple-element.25), channel_id=1, source_target_pairs={{4,0},{8,4},{12,8},{5,1},{9,5},{13,9},{6,2},{10,6},{14,10},{7,3},{... | collective-permute-start | bytes 122888 | tf_op jit(solution)/shard_map/ppermute | solution.py:15
  19.8 33.9 %collective-permute-start.4 = (bf16[80,1,384]{0,2,1:T(8,128)(2,1)}, bf16[80,1,384]{0,2,1:T(8,128)(2,1)S(1)}, u32[]{:S(2)}, u32[]{:S(2)}) collective-permute-start(bf16[80,1,384]{0,2,1:T(8,128)(2,1)} %get-tuple-element.22), channel_id=1, source_target_pairs={{0,4},{4,8},{8,12},{1,5},{5,9},{9,13},{2,6},{6,10},{10,14},{3,7},{... | collective-permute-start | bytes 184328 | tf_op jit(solution)/shard_map/ppermute | solution.py:12
  23.8 29.9 %collective-permute-start.5 = (bf16[80,1,384]{0,2,1:T(8,128)(2,1)S(1)}, bf16[80,1,384]{0,2,1:T(8,128)(2,1)S(1)}, u32[]{:S(2)}, u32[]{:S(2)}) collective-permute-start(bf16[80,1,384]{0,2,1:T(8,128)(2,1)S(1)} %get-tuple-element.23), channel_id=1, source_target_pairs={{4,0},{8,4},{12,8},{5,1},{9,5},{13,9},{6,2},{10,6},{14,10},{7,3},{... | collective-permute-start | bytes 184328 | tf_op jit(solution)/shard_map/ppermute | solution.py:15
  27.0 9.1 %collective-permute-start.2 = (bf16[80,10,1]{2,1,0:T(8,128)(2,1)S(1)}, bf16[80,10,1]{2,1,0:T(8,128)(2,1)S(1)}, u32[]{:S(2)}, u32[]{:S(2)}) collective-permute-start(bf16[80,10,1]{2,1,0:T(8,128)(2,1)S(1)} %get-tuple-element.16), channel_id=1, source_target_pairs={{0,1},{1,2},{2,3},{4,5},{5,6},{6,7},{8,9},{9,10},{10,11},{12,13},{... | collective-permute-start | bytes 4808 | tf_op jit(solution)/shard_map/ppermute | solution.py:12
  32.1 8.4 %collective-permute-start.3 = (bf16[80,10,1]{2,1,0:T(8,128)(2,1)S(1)}, bf16[80,10,1]{2,1,0:T(8,128)(2,1)S(1)}, u32[]{:S(2)}, u32[]{:S(2)}) collective-permute-start(bf16[80,10,1]{2,1,0:T(8,128)(2,1)S(1)} %get-tuple-element.17), channel_id=1, source_target_pairs={{1,0},{2,1},{3,2},{5,4},{6,5},{7,6},{9,8},{10,9},{11,10},{13,12},{... | collective-permute-start | bytes 4808 | tf_op jit(solution)/shard_map/ppermute | solution.py:15
  34.1 7.5 %copy-start.15 = (f32[80]{0:T(128)S(1)}, f32[80]{0:T(128)}, u32[]{:S(2)}) copy-start(f32[80]{0:T(128)} %param.12) | copy-start | bytes 964
  47.6 14.2 %all-to-all-start.1 = ((f32[80,4,256]{2,0,1:T(8,128)}), f32[80,4,256]{2,0,1:T(8,128)S(1)}, u32[]{:S(2)}, u32[]{:S(2)}) async-start(f32[80,4,256]{2,0,1:T(8,128)} %broadcast_select_fusion), calls=%async_computation.1 | async-start | bytes 655360 | tf_op jit(solution)/shard_map/all_to_all | solution.py:84
  53.7 4.4 %collective-permute-start.6 = (bf16[80,8,1]{0,2,1:T(2,128)(2,1)S(1)}, bf16[80,8,1]{0,2,1:T(2,128)(2,1)S(1)}, u32[]{:S(2)}, u32[]{:S(2)}) collective-permute-start(bf16[80,8,1]{0,2,1:T(2,128)(2,1)S(1)} %get-tuple-element.14), channel_id=1, source_target_pairs={{0,1},{1,2},{2,3},{4,5},{5,6},{6,7},{8,9},{9,10},{10,11},{12,13},{... | collective-permute-start | bytes 3848 | tf_op jit(solution)/shard_map/ppermute | solution.py:12
  55.7 4.9 %collective-permute-start.7 = (bf16[80,8,1]{0,2,1:T(2,128)(2,1)S(1)}, bf16[80,8,1]{0,2,1:T(2,128)(2,1)S(1)}, u32[]{:S(2)}, u32[]{:S(2)}) collective-permute-start(bf16[80,8,1]{0,2,1:T(2,128)(2,1)S(1)} %get-tuple-element.15), channel_id=1, source_target_pairs={{1,0},{2,1},{3,2},{5,4},{6,5},{7,6},{9,8},{10,9},{11,10},{13,12},{... | collective-permute-start | bytes 3848 | tf_op jit(solution)/shard_map/ppermute | solution.py:15
  71.9 5.3 %collective-permute-start.8 = (bf16[80,1,384]{0,2,1:T(8,128)(2,1)S(1)}, bf16[80,1,384]{0,2,1:T(8,128)(2,1)S(1)}, u32[]{:S(2)}, u32[]{:S(2)}) collective-permute-start(bf16[80,1,384]{0,2,1:T(8,128)(2,1)S(1)} %get-tuple-element.20), channel_id=1, source_target_pairs={{0,4},{4,8},{8,12},{1,5},{5,9},{9,13},{2,6},{6,10},{10,14},{3,7},{... | collective-permute-start | bytes 184328 | tf_op jit(solution)/shard_map/ppermute | solution.py:12
  75.5 5.4 %collective-permute-start.9 = (bf16[80,1,384]{0,2,1:T(8,128)(2,1)S(1)}, bf16[80,1,384]{0,2,1:T(8,128)(2,1)S(1)}, u32[]{:S(2)}, u32[]{:S(2)}) collective-permute-start(bf16[80,1,384]{0,2,1:T(8,128)(2,1)S(1)} %get-tuple-element.21), channel_id=1, source_target_pairs={{4,0},{8,4},{12,8},{5,1},{9,5},{13,9},{6,2},{10,6},{14,10},{7,3},{... | collective-permute-start | bytes 184328 | tf_op jit(solution)/shard_map/ppermute | solution.py:15
  81.0 5.5 %collective-permute-start.10 = (bf16[80,8,1]{0,2,1:T(2,128)(2,1)S(1)}, bf16[80,8,1]{0,2,1:T(2,128)(2,1)S(1)}, u32[]{:S(2)}, u32[]{:S(2)}) collective-permute-start(bf16[80,8,1]{0,2,1:T(2,128)(2,1)S(1)} %get-tuple-element.12), channel_id=1, source_target_pairs={{0,1},{1,2},{2,3},{4,5},{5,6},{6,7},{8,9},{9,10},{10,11},{12,13},{... | collective-permute-start | bytes 3848 | tf_op jit(solution)/shard_map/ppermute | solution.py:12
  84.3 5.2 %copy-start.9 = (f32[6]{0:T(128)S(1)}, f32[6]{0:T(128)}, u32[]{:S(2)}) copy-start(f32[6]{0:T(128)} %get-tuple-element.26) | copy-start | bytes 76
  84.3 5.2 %copy-start.10 = (f32[6]{0:T(128)S(1)}, f32[6]{0:T(128)}, u32[]{:S(2)}) copy-start(f32[6]{0:T(128)} %get-tuple-element.27) | copy-start | bytes 76
  84.3 5.2 %copy-start.11 = (f32[80]{0:T(128)S(1)}, f32[80]{0:T(128)}, u32[]{:S(2)}) copy-start(f32[80]{0:T(128)} %param.14) | copy-start | bytes 964
  84.4 4.9 %collective-permute-start.11 = (bf16[80,8,1]{0,2,1:T(2,128)(2,1)S(1)}, bf16[80,8,1]{0,2,1:T(2,128)(2,1)S(1)}, u32[]{:S(2)}, u32[]{:S(2)}) collective-permute-start(bf16[80,8,1]{0,2,1:T(2,128)(2,1)S(1)} %get-tuple-element.13), channel_id=1, source_target_pairs={{1,0},{2,1},{3,2},{5,4},{6,5},{7,6},{9,8},{10,9},{11,10},{13,12},{... | collective-permute-start | bytes 3848 | tf_op jit(solution)/shard_map/ppermute | solution.py:15
  94.0 13.9 %copy-start.8 = (s32[256]{0:T(256)S(1)}, s32[256]{0:T(256)}, u32[]{:S(2)}) copy-start(s32[256]{0:T(256)} %copy-done.7) | copy-start | bytes 3076
  94.1 4.7 %collective-permute-start.12 = (bf16[80,1,384]{0,2,1:T(8,128)(2,1)S(1)}, bf16[80,1,384]{0,2,1:T(8,128)(2,1)S(1)}, u32[]{:S(2)}, u32[]{:S(2)}) collective-permute-start(bf16[80,1,384]{0,2,1:T(8,128)(2,1)S(1)} %get-tuple-element.18), channel_id=1, source_target_pairs={{0,4},{4,8},{8,12},{1,5},{5,9},{9,13},{2,6},{6,10},{10,14},{3,7},{... | collective-permute-start | bytes 184328 | tf_op jit(solution)/shard_map/ppermute | solution.py:12
  97.2 5.4 %collective-permute-start.13 = (bf16[80,1,384]{0,2,1:T(8,128)(2,1)S(1)}, bf16[80,1,384]{0,2,1:T(8,128)(2,1)S(1)}, u32[]{:S(2)}, u32[]{:S(2)}) collective-permute-start(bf16[80,1,384]{0,2,1:T(8,128)(2,1)S(1)} %get-tuple-element.19), channel_id=1, source_target_pairs={{4,0},{8,4},{12,8},{5,1},{9,5},{13,9},{6,2},{10,6},{14,10},{7,3},{... | collective-permute-start | bytes 184328 | tf_op jit(solution)/shard_map/ppermute | solution.py:15
  102.6 5.3 %collective-permute-start.14 = (bf16[80,8,1]{0,2,1:T(2,128)(2,1)S(1)}, bf16[80,8,1]{0,2,1:T(2,128)(2,1)S(1)}, u32[]{:S(2)}, u32[]{:S(2)}) collective-permute-start(bf16[80,8,1]{0,2,1:T(2,128)(2,1)S(1)} %get-tuple-element.10), channel_id=1, source_target_pairs={{0,1},{1,2},{2,3},{4,5},{5,6},{6,7},{8,9},{9,10},{10,11},{12,13},{... | collective-permute-start | bytes 3848 | tf_op jit(solution)/shard_map/ppermute | solution.py:12
  106.0 4.9 %collective-permute-start.15 = (bf16[80,8,1]{0,2,1:T(2,128)(2,1)S(1)}, bf16[80,8,1]{0,2,1:T(2,128)(2,1)S(1)}, u32[]{:S(2)}, u32[]{:S(2)}) collective-permute-start(bf16[80,8,1]{0,2,1:T(2,128)(2,1)S(1)} %get-tuple-element.11), channel_id=1, source_target_pairs={{1,0},{2,1},{3,2},{5,4},{6,5},{7,6},{9,8},{10,9},{11,10},{13,12},{... | collective-permute-start | bytes 3848 | tf_op jit(solution)/shard_map/ppermute | solution.py:15
  114.9 6.0 %copy-start.3 = (f32[2048,80]{0,1:T(8,128)S(1)}, f32[2048,80]{0,1:T(8,128)}, u32[]{:S(2)}) copy-start(f32[2048,80]{0,1:T(8,128)} %copy-done.2) | copy-start | bytes 1966084
  117.4 12.6 %all-to-all-start.2 = ((f32[80,4,256]{2,0,1:T(8,128)}), f32[80,4,256]{2,0,1:T(8,128)S(1)}, u32[]{:S(2)}, u32[]{:S(2)}) async-start(f32[80,4,256]{2,0,1:T(8,128)} %copy.84), calls=%async_computation.2 | async-start | bytes 655360 | tf_op jit(solution)/shard_map/all_to_all | solution.py:107
  130.2 7.5 %copy-start.16 = (f32[80]{0:T(128)S(1)}, f32[80]{0:T(128)}, u32[]{:S(2)}) copy-start(f32[80]{0:T(128)} %param.15) | copy-start | bytes 964
  (4 other events, 13.7 us)
where the time goes:
time: 140 us; the launch traced here: 139 us
  starting transfers between devices  55.6 us (40%)
  waiting for transfers between devices  31.1 us (22%)
  local copies, waits for them, and re-layouts  22.6 us (16%)
  other arithmetic  21.1 us (15%)
  matrix products  6.69 us (5%)
    ppermute x8, starting transfers between devices, extended(): lax.ppermute(lax.slice_in_dim(block, block.shape[dim] - width, None, axis...  27.9 us
    ppermute x8, waiting for transfers between devices, extended(): lax.ppermute(lax.slice_in_dim(block, 0, width, axis=dim), axis, backward)  20.3 us
    ppermute x8, starting transfers between devices, extended(): lax.ppermute(lax.slice_in_dim(block, 0, width, axis=dim), axis, backward)  13.4 us
    all_to_all x1, waiting for transfers between devices, body(): lax.all_to_all(outgoing, 'gx', split_axis=1, concat_axis=1, tiled=True)  8.16 us
    scatter-add x1, other arithmetic, body(): summed = jnp.zeros_like(flat_parent).at[:, served_ids].add(incoming)  7.06 us
    dot_general x4, matrix products, mix_levels(): jnp.dot(matrix, flat_values, precision=lax.Precision.HIGHEST, preferred_e...  6.69 us
    all_to_all x1, starting transfers between devices, body(): lax.all_to_all(jnp.take(flat_parent, served_ids, axis=1), 'gx', split_axi...  5.43 us
    all_to_all x1, starting transfers between devices, body(): lax.all_to_all(wanted, 'gx', split_axis=0, concat_axis=0, tiled=True)  5.42 us
  transfers between devices with their start and end apart: 19, of which 10 were waited for; matrix products, arithmetic and copies ran while one was open for 11% of the time, Pallas kernels for 0%

commit v1 on v0

v1 whole, which is shorter than its diff:
```python
import functools

import jax
import jax.numpy as jnp
from jax import lax
from jax.experimental import pallas as pl
from jax.experimental.pallas import tpu as pltpu
from jax.sharding import PartitionSpec as P

MESH = pl.DeviceIdType.MESH
F32 = jnp.float32
BF16 = jnp.bfloat16
LOW, HIGH = 0, 1
TURNS = 3


def dot(a, b):
    return jnp.dot(a, b, preferred_element_type=F32)


def one_hot(mask):
    return jnp.where(mask, 1.0, 0.0).astype(BF16)


def split(x):
    high = x.astype(BF16)
    return high, (x - high.astype(F32)).astype(BF16)


def over(first, count, step):
    if count <= 8:
        for k in range(first, count):
            step(k)
    else:
        lax.fori_loop(first, count, lambda k, _: (step(k), 0)[1], 0)


def kernel(
    n_x, n_gy, n_gz,
    parent, nest, nu_p, nu_n, relax, feedback, vert_mix, owner, cell, nest_of,
    parent_out, nest_out,
    keys, prow, pcol, pcol_send, nrow, nrow_send, ncol, ncol_send,
    state, stepped, stepped_bf, answers, answers_send, means, lhs, pulled,
    row_s, row_r, col_s, col_r, key_s, key_r, ans_s, ans_r, mean_s, mean_r,
):
    prows, levels, pcols = parent.shape
    nrows, _, ncols = nest.shape
    brows, bcols = nrows // 3, ncols // 3
    blocks = brows * bcols
    total_rows = nest_of.shape[0]
    me = lax.axis_index("gx")
    tile = lax.axis_index("gy") * n_gz + lax.axis_index("gz")
    n_y = n_gy * n_gz

    def y_device(t):
        return {"gy": t // n_gz, "gz": t % n_gz}

    x_side = ((me > 0, {"gx": me - 1}), (me < n_x - 1, {"gx": me + 1}))
    y_side = ((tile > 0, y_device(tile - 1)), (tile < n_y - 1, y_device(tile + 1)))

    barrier = pltpu.get_barrier_semaphore()

    def greet(k):
        pl.semaphore_signal(
            barrier, inc=1, device_id={"gx": lax.rem(me + k, n_x)}, device_id_type=MESH
        )

    over(1, n_x, greet)
    for present, device in y_side:
        @pl.when(present)
        def _():
            pl.semaphore_signal(barrier, inc=1, device_id=device, device_id_type=MESH)

    lane128 = lax.broadcasted_iota(jnp.int32, (levels, 128), 1)

    def pack(columns):
        packed = jnp.zeros((levels, 128), F32)
        for r, column in enumerate(columns):
            packed = jnp.where(lane128 == r, column, packed)
        return packed.astype(BF16)

    def edges(rows, width):
        low = pack([rows[r][:, 0:1] for r in range(len(rows))])
        high = pack([rows[r][:, width - 1:width] for r in range(len(rows))])
        return low, high

    p = [parent[r].astype(F32) for r in range(prows)]
    for side, packed in enumerate(edges(p, pcols)):
        pcol_send[side] = packed
    s = [nest[r].astype(F32) for r in range(nrows)]
    for side, packed in enumerate(edges(s, ncols)):
        ncol_send[0, side] = packed
    key = owner[...] * (prows * pcols) + cell[...]
    keys[0] = jnp.broadcast_to(key, keys.shape[1:])

    for side in (LOW, HIGH):
        @pl.when(jnp.logical_not(x_side[side][0]))
        def _():
            prow[side] = jnp.zeros(prow.shape[1:], BF16)
            for turn in range(TURNS):
                nrow[turn, side] = jnp.zeros(nrow.shape[2:], BF16)

        @pl.when(jnp.logical_not(y_side[side][0]))
        def _():
            pcol[side] = jnp.zeros(pcol.shape[1:], BF16)
            for turn in range(TURNS):
                ncol[turn, side] = jnp.zeros(ncol.shape[2:], BF16)

    callers = n_x - 1 + sum(present.astype(jnp.int32) for present, _ in y_side)
    pl.semaphore_wait(barrier, callers)

    def copy(src, dst, send_sem, recv_sem, device):
        return pltpu.make_async_remote_copy(
            src_ref=src, dst_ref=dst, send_sem=send_sem, recv_sem=recv_sem,
            device_id=device, device_id_type=MESH,
        )

    def halo(sides, side, src, dst, send_sems, recv_sems, which, do):
        present, device = sides[side]

        @pl.when(present)
        def _():
            if do == "start":
                copy(src, dst(1 - side), send_sems.at[which, side],
                     recv_sems.at[which, 1 - side], device).start()
            elif do == "recv":
                copy(src, dst(side), send_sems.at[which, side],
                     recv_sems.at[which, side], device).wait_recv()
            else:
                copy(src, dst(1 - side), send_sems.at[which, side],
                     recv_sems.at[which, 1 - side], device).wait_send()

    def parent_halo(side, do):
        halo(x_side, side, parent.at[0 if side == LOW else prows - 1],
             lambda where: prow.at[where], row_s, row_r, 0, do)
        halo(y_side, side, pcol_send.at[side], lambda where: pcol.at[where], col_s, col_r, 0, do)

    def nest_halo(turn, side, do, kinds=("x", "y")):
        if "x" in kinds:
            if turn == 0:
                src = nest.at[0 if side == LOW else nrows - 1]
            else:
                src = nrow_send.at[turn - 1, side]
            halo(x_side, side, src, lambda where: nrow.at[turn, where], row_s, row_r, 1 + turn, do)
        if "y" in kinds:
            halo(y_side, side, ncol_send.at[turn, side], lambda where: ncol.at[turn, where],
                 col_s, col_r, 1 + turn, do)

    def peer(k):
        return {"gx": lax.rem(me + k, n_x)}

    def key_copy(k):
        return copy(keys.at[0], keys.at[k], key_s.at[k], key_r.at[k], peer(k))

    def answer_copy(k):
        return copy(answers_send.at[k], answers.at[k], ans_s.at[k], ans_r.at[k],
                    {"gx": lax.rem(me + (n_x - k), n_x)})

    def mean_copy(k):
        return copy(means.at[0], means.at[k], mean_s.at[k], mean_r.at[k], peer(k))

    for side in (LOW, HIGH):
        parent_halo(side, "start")
    over(1, n_x, lambda k: key_copy(k).start())
    for side in (LOW, HIGH):
        nest_halo(0, side, "start")

    def level_column(ref):
        at = lax.broadcasted_iota(jnp.int32, (levels, levels), 0)
        across = lax.broadcasted_iota(jnp.int32, (levels, levels), 1)
        return jnp.sum(jnp.where(at == across, ref[...], 0.0), axis=1, keepdims=True)

    nu_parent_c, nu_nest_c = level_column(nu_p), level_column(nu_n)
    relax_c, feedback_c = level_column(relax), level_column(feedback)
    keep_c = 1.0 - relax_c

    m_high, m_low = split(vert_mix[...])
    wide_at = lax.broadcasted_iota(jnp.int32, (levels, 3 * levels), 0)
    wide_across = lax.broadcasted_iota(jnp.int32, (levels, 3 * levels), 1)
    place_high = one_hot((wide_across == wide_at) | (wide_across == wide_at + levels))
    place_low = one_hot(wide_across == wide_at + 2 * levels)
    lhs[...] = (dot(m_high, place_high) + dot(m_low, place_low)).astype(BF16)

    def mix(x):
        high, low = split(x)
        return dot(lhs[...], jnp.concatenate([high, low, high], axis=0))

    def beside(x, low, high, width):
        lane = lax.broadcasted_iota(jnp.int32, (levels, width), 1)
        before = jnp.where(lane == 0, low, pltpu.roll(x, 1, axis=1))
        after = jnp.where(lane == width - 1, high, pltpu.roll(x, width - 1, axis=1))
        return before + after

    for side in (LOW, HIGH):
        parent_halo(side, "recv")
    p_low, p_high = pcol[LOW].astype(F32), pcol[HIGH].astype(F32)
    for r in range(prows):
        centre = parent[r].astype(F32)
        above = (parent[r - 1] if r > 0 else prow[LOW]).astype(F32)
        below = (parent[r + 1] if r < prows - 1 else prow[HIGH]).astype(F32)
        around = above + below + beside(centre, p_low[:, r:r + 1], p_high[:, r:r + 1], pcols)
        out = mix(centre + nu_parent_c * (around - 4.0 * centre))
        stepped[r] = out
        stepped_bf[r * levels:(r + 1) * levels, :] = out.astype(BF16)

    parent_col = lax.broadcasted_iota(jnp.int32, (pcols, blocks), 0)
    shift = pcols.bit_length() - 1

    def places(k):
        here = keys[k, 0:1, :] - me * (prows * pcols)
        return lax.shift_right_arithmetic(here, shift), one_hot(parent_col == (here & (pcols - 1)))

    def serve(k):
        if not (isinstance(k, int) and k == 0):
            key_copy(k).wait_recv()
        row, hot = places(k)
        found = dot(stepped_bf[...], hot)
        total = jnp.zeros((levels, blocks), F32)
        for r in range(prows):
            total = jnp.where(row == r, found[r * levels:(r + 1) * levels], total)
        if isinstance(k, int) and k == 0:
            answers[0] = total.astype(BF16)
        else:
            answers_send[k] = total.astype(BF16)
            answer_copy(k).start()

    over(1, n_x, serve)
    serve(0)

    def weight(low_row):
        first = nest_of[lax.rem(low_row + total_rows, total_rows)]
        second = nest_of[lax.rem(low_row + 1, total_rows)]
        return jnp.where(first == second, 1.0, 0.0).astype(F32)

    weights = [weight(me * nrows + r - 1) for r in range(nrows + 1)]

    def diffuse(turn, get, put):
        low, high = ncol[turn, LOW].astype(F32), ncol[turn, HIGH].astype(F32)
        for r in range(nrows):
            centre = get(r)
            above = get(r - 1) if r > 0 else nrow[turn, LOW].astype(F32)
            below = get(r + 1) if r < nrows - 1 else nrow[turn, HIGH].astype(F32)
            around = (
                above * weights[r] + below * weights[r + 1]
                + beside(centre, low[:, r:r + 1], high[:, r:r + 1], ncols)
            )
            put(r, mix(keep_c * (centre + nu_nest_c * (around - 4.0 * centre))))

    for side in (LOW, HIGH):
        nest_halo(0, side, "recv")

    def put_state(r, value):
        state[0, r] = value

    diffuse(0, lambda r: nest[r].astype(F32), put_state)

    parent_row = lax.broadcasted_iota(jnp.int32, (16, blocks), 0)

    def count_step(k):
        row, hot = places(k)
        return lax.dot_general(
            one_hot(parent_row == row), hot, (((1,), (1,)), ((), ())), preferred_element_type=F32
        )

    forced = answers[0].astype(F32)
    if n_x <= 8:
        counts = count_step(0)
        for k in range(1, n_x):
            counts = counts + count_step(k)
        for k in range(1, n_x):
            answer_copy(k).wait_recv()
            forced = forced + answers[k].astype(F32)
    else:
        counts = lax.fori_loop(
            0, n_x, lambda k, t: t + count_step(k), jnp.zeros((16, pcols), F32))

        def collect(k, t):
            answer_copy(k).wait_recv()
            return t + answers[k].astype(F32)

        forced = lax.fori_loop(1, n_x, collect, forced)

    block_at = lax.broadcasted_iota(jnp.int32, (bcols, ncols), 0)
    cell_at = lax.broadcasted_iota(jnp.int32, (bcols, ncols), 1)
    spread = one_hot((cell_at >= 3 * block_at) & (cell_at < 3 * block_at + 3))
    spread2 = jnp.concatenate([spread, spread], axis=0)
    drive = mix(relax_c * forced)
    for a in range(brows):
        high, low = split(drive[:, a * bcols:(a + 1) * bcols])
        pulled[a] = dot(jnp.concatenate([high, low], axis=1), spread2)

    def send_rows(turn, r, value):
        if r == 0:
            nrow_send[turn - 1, LOW] = value.astype(BF16)
            nest_halo(turn, LOW, "start", ("x",))
        if r == nrows - 1:
            nrow_send[turn - 1, HIGH] = value.astype(BF16)
            nest_halo(turn, HIGH, "start", ("x",))

    def send_cols(turn, slot):
        rows = [state[slot, r] for r in range(nrows)]
        for side, packed in enumerate(edges(rows, ncols)):
            ncol_send[turn, side] = packed
            nest_halo(turn, side, "start", ("y",))

    for r in (0, nrows - 1, *range(1, nrows - 1)):
        value = state[0, r] + pulled[r // 3]
        state[0, r] = value
        send_rows(1, r, value)
    send_cols(1, 0)

    for turn in range(1, TURNS):
        for side in (LOW, HIGH):
            nest_halo(turn, side, "recv")
        now, later = (turn - 1) % 2, turn % 2

        def put_next(r, value):
            value = value + pulled[r // 3]
            state[later, r] = value
            if turn < TURNS - 1:
                send_rows(turn + 1, r, value)
            else:
                nest_out[r] = value.astype(BF16)

        diffuse(turn, lambda r: state[now, r], put_next)
        if turn < TURNS - 1:
            send_cols(turn + 1, later)

    last = (TURNS - 1) % 2
    for a in range(brows):
        summed = state[last, 3 * a] + state[last, 3 * a + 1] + state[last, 3 * a + 2]
        high, low = split(summed)
        both = lax.dot_general(
            jnp.concatenate([high, low], axis=0), spread,
            (((1,), (1,)), ((), ())), preferred_element_type=F32,
        )
        mean = (both[:levels] + both[levels:]) * (1.0 / 9.0)
        means[0, :, a * bcols:(a + 1) * bcols] = mean.astype(BF16)
    over(1, n_x, lambda k: mean_copy(k).start())

    def give(k, total):
        row, hot = places(k)
        mean = means[k].astype(F32)
        shared = jnp.concatenate(
            [jnp.where(row == r, mean, 0.0).astype(BF16) for r in range(prows)], axis=0
        )
        return total + lax.dot_general(
            shared, hot, (((1,), (1,)), ((), ())), preferred_element_type=F32)

    returned = give(0, jnp.zeros((prows * levels, pcols), F32))
    if n_x <= 8:
        for k in range(1, n_x):
            mean_copy(k).wait_recv()
            returned = give(k, returned)
    else:
        def give_next(k, total):
            mean_copy(k).wait_recv()
            return give(k, total)

        returned = lax.fori_loop(1, n_x, give_next, returned)
    for r in range(prows):
        own = stepped[r]
        back = returned[r * levels:(r + 1) * levels] - counts[r:r + 1, :] * own
        parent_out[r] = (own + feedback_c * back).astype(BF16)

    for side in (LOW, HIGH):
        parent_halo(side, "send")
        for turn in range(TURNS):
            nest_halo(turn, side, "send")

    def sent(k):
        key_copy(k).wait_send()
        answer_copy(k).wait_send()
        mean_copy(k).wait_send()

    over(1, n_x, sent)


def body(n_x, n_gy, n_gz, parent, nest, nu_p, nu_n, relax, feedback, vert_mix, owner, cell, nest_of):
    levels, prows, pcols = parent.shape
    _, nrows, ncols = nest.shape
    blocks = cell.size
    vmem = pl.BlockSpec(memory_space=pltpu.VMEM)
    smem = pl.BlockSpec(memory_space=pltpu.SMEM)
    dma = pltpu.SemaphoreType.DMA
    parent_out, nest_out = pl.pallas_call(
        functools.partial(kernel, n_x, n_gy, n_gz),
        out_shape=(
            jax.ShapeDtypeStruct((prows, levels, pcols), BF16),
            jax.ShapeDtypeStruct((nrows, levels, ncols), BF16),
        ),
        in_specs=[vmem] * 9 + [smem],
        out_specs=(vmem, vmem),
        scratch_shapes=[
            pltpu.VMEM((n_x, 8, blocks), jnp.int32),
            pltpu.VMEM((2, levels, pcols), BF16),
            pltpu.VMEM((2, levels, 128), BF16),
            pltpu.VMEM((2, levels, 128), BF16),
            pltpu.VMEM((TURNS, 2, levels, ncols), BF16),
            pltpu.VMEM((TURNS - 1, 2, levels, ncols), BF16),
            pltpu.VMEM((TURNS, 2, levels, 128), BF16),
            pltpu.VMEM((TURNS, 2, levels, 128), BF16),
            pltpu.VMEM((2, nrows, levels, ncols), F32),
            pltpu.VMEM((prows, levels, pcols), F32),
            pltpu.VMEM((prows * levels, pcols), BF16),
            pltpu.VMEM((n_x, levels, blocks), BF16),
            pltpu.VMEM((n_x, levels, blocks), BF16),
            pltpu.VMEM((n_x, levels, blocks), BF16),
            pltpu.VMEM((levels, 3 * levels), BF16),
            pltpu.VMEM((nrows // 3, levels, ncols), F32),
            dma((1 + TURNS, 2)), dma((1 + TURNS, 2)), dma((1 + TURNS, 2)), dma((1 + TURNS, 2)),
            dma((n_x,)), dma((n_x,)), dma((n_x,)), dma((n_x,)), dma((n_x,)), dma((n_x,)),
        ],
        compiler_params=pltpu.CompilerParams(
            collective_id=0, has_side_effects=True, vmem_limit_bytes=40 * 1024 * 1024
        ),
    )(
        parent.transpose(1, 0, 2), nest.transpose(1, 0, 2),
        nu_p.reshape(1, -1), nu_n.reshape(1, -1), relax.reshape(1, -1), feedback.reshape(1, -1),
        vert_mix, owner.reshape(1, -1), cell.reshape(1, -1), nest_of,
    )
    return parent_out.transpose(1, 0, 2), nest_out.transpose(1, 0, 2)


def solution(mesh):
    sizes = mesh.shape
    grid = P("groups", "gx", ("gy", "gz"))
    placed = (
        grid, grid, P(), P(), P(), P(), P(),
        P("gx", ("gy", "gz"), None, None), P("gx", ("gy", "gz"), None), P(),
    )
    return jax.shard_map(
        functools.partial(body, sizes["gx"], sizes["gy"], sizes["gz"]),
        mesh=mesh,
        in_specs=placed,
        out_specs=(grid, grid),
        check_vma=False,
    )
```

time: 140 us -> 34.3 us (0.24)
  the two profiles are of different devices: /device:TPU:1 before, /device:TPU:0 now
where the time goes in v1:
time: 34.3 us; the launch traced here: 34.1 us
  Pallas kernels  30.1 us (88%)
  local copies, waits for them, and re-layouts  3.26 us (10%)
  between operations  0.77 us (2%)
    pallas_call x1, Pallas kernels, body(): pl.pallas_call(functools.partial(kernel, n_x, n_gy, n_gz), out_shape=(jax...  30.1 us
    unnamed x21, local copies, waits for them, and re-layouts  3.26 us

profile of v1, /device:TPU:0, one launch (start us, length us, event | category | flops | bytes accessed | tf_op | source)
XLA Modules:
  0.0 34.1 jit_solution(4511679699808948093)
XLA Ops:
  0.6 0.0 copy-start
  0.6 0.0 copy-start.1
  0.7 0.0 copy-start.3
  0.7 0.0 copy-start.5
  0.7 0.0 copy-start.6
  0.7 0.0 copy-start.7
  0.7 0.0 copy-start.8
  0.7 1.1 %copy.15 = bf16[80,8,256]{2,0,1:T(8,128)(2,1)S(1)} copy(bf16[80,8,256]{2,1,0:T(8,128)(2,1)} %param.10) | data formatting | bytes 655360 | tf_op args[0]
  1.8 0.0 copy-start.2
  1.8 0.0 copy-start.4
  1.8 0.0 copy-done
  1.8 0.0 copy-done.1
  1.8 0.0 copy-done.3
  1.8 0.0 copy-done.5
  1.8 0.0 copy-done.6
  1.9 0.0 copy-done.7
  1.9 0.0 copy-done.8
  1.9 0.6 %copy-done.2 = s32[1,1,256,1]{2,3,1,0:T(1,128)S(1)} copy-done((s32[1,1,256,1]{2,3,1,0:T(1,128)S(1)}, s32[1,1,256,1]{2,3,1,0:T(1,128)}, u32[]{:S(2)}) %copy-start.2) | copy-done | bytes 1048
  2.5 0.0 copy-done.4
  2.5 30.1 %shard_map.113 = (bf16[8,80,256]{2,1,0:T(8,128)(2,1)S(1)}, bf16[6,80,384]{2,1,0:T(8,128)(2,1)S(1)}) custom-call(bf16[8,80,256]{2,1,0:T(8,128)(2,1)S(1)} %bitcast.12, bf16[6,80,384]{2,1,0:T(8,128)(2,1)S(1)} %bitcast.13, f32[1,80]{1,0:T(1,128)S(1)} %bitcast.18, f32[1,80]{1,0:T(1,128)S(1)} %bitcast.19, f32[1,80]{1,0:T(1,128)S(1)} %bitcast.20, ...), custom_call_target="tpu_custom_call" | custom-call | tf_op jit(solution)/shard_map/pallas_call | solution.py:386
  32.6 0.8 %copy.13 = bf16[80,8,256]{2,1,0:T(8,128)(2,1)} copy(bf16[80,8,256]{2,0,1:T(8,128)(2,1)S(1)} %bitcast.15) | data formatting | bytes 655360
  33.4 0.7 %copy.17 = bf16[80,6,384]{2,0,1:T(8,128)(2,1)} copy(bf16[80,6,384]{2,0,1:T(8,128)(2,1)S(1)} %bitcast.14) | data formatting | bytes 737280
Async XLA Ops:
  0.6 1.2 %copy-start = (bf16[80,6,384]{2,0,1:T(8,128)(2,1)S(1)}, bf16[80,6,384]{2,0,1:T(8,128)(2,1)}, u32[]{:S(2)}) copy-start(bf16[80,6,384]{2,0,1:T(8,128)(2,1)} %param.11) | copy-start | bytes 1105924
  0.6 1.2 %copy-start.1 = (f32[80,80]{1,0:T(8,128)S(1)}, f32[80,80]{1,0:T(8,128)}, u32[]{:S(2)}) copy-start(f32[80,80]{1,0:T(8,128)} %vert_mix.1) | copy-start | bytes 76804
  0.7 1.2 %copy-start.3 = (s32[1,1,256]{2,1,0:T(1,128)S(1)}, s32[1,1,256]{2,1,0:T(1,128)}, u32[]{:S(2)}) copy-start(s32[1,1,256]{2,1,0:T(1,128)} %param.18) | copy-start | bytes 3076
  0.7 1.2 %copy-start.5 = (f32[80]{0:T(128)S(1)}, f32[80]{0:T(128)}, u32[]{:S(2)}) copy-start(f32[80]{0:T(128)} %param.13) | copy-start | bytes 964
  0.7 1.2 %copy-start.6 = (f32[80]{0:T(128)S(1)}, f32[80]{0:T(128)}, u32[]{:S(2)}) copy-start(f32[80]{0:T(128)} %param.14) | copy-start | bytes 964
  0.7 1.2 %copy-start.7 = (f32[80]{0:T(128)S(1)}, f32[80]{0:T(128)}, u32[]{:S(2)}) copy-start(f32[80]{0:T(128)} %param.15) | copy-start | bytes 964
  0.7 1.2 %copy-start.8 = (s32[24]{0:T(128)S(1)}, s32[24]{0:T(128)}, u32[]{:S(2)}) copy-start(s32[24]{0:T(128)} %nest_of.1) | copy-start | bytes 292
  1.8 0.7 %copy-start.2 = (s32[1,1,256,1]{2,3,1,0:T(1,128)S(1)}, s32[1,1,256,1]{2,3,1,0:T(1,128)}, u32[]{:S(2)}) copy-start(s32[1,1,256,1]{2,3,1,0:T(1,128)} %param.17) | copy-start | bytes 3076
  1.8 0.7 %copy-start.4 = (f32[80]{0:T(128)S(1)}, f32[80]{0:T(128)}, u32[]{:S(2)}) copy-start(f32[80]{0:T(128)} %param.12) | copy-start | bytes 964

commit v2 on v1

--- a/solution.py
+++ b/solution.py
@@ -40,7 +40,7 @@
     parent, nest, nu_p, nu_n, relax, feedback, vert_mix, owner, cell, nest_of,
     parent_out, nest_out,
     keys, prow, pcol, pcol_send, nrow, nrow_send, ncol, ncol_send,
-    state, stepped, stepped_bf, answers, answers_send, means, lhs, pulled,
+    state, stepped, stepped_bf, answers, answers_send, means, lhs, pulled, back,
     row_s, row_r, col_s, col_r, key_s, key_r, ans_s, ans_r, mean_s, mean_r,
 ):
     prows, levels, pcols = parent.shape
@@ -77,7 +77,7 @@
         packed = jnp.zeros((levels, 128), F32)
         for r, column in enumerate(columns):
             packed = jnp.where(lane128 == r, column, packed)
-        return packed.astype(BF16)
+        return packed
 
     def edges(rows, width):
         low = pack([rows[r][:, 0:1] for r in range(len(rows))])
@@ -86,10 +86,10 @@
 
     p = [parent[r].astype(F32) for r in range(prows)]
     for side, packed in enumerate(edges(p, pcols)):
-        pcol_send[side] = packed
+        pcol_send[side] = packed.astype(BF16)
     s = [nest[r].astype(F32) for r in range(nrows)]
     for side, packed in enumerate(edges(s, ncols)):
-        ncol_send[0, side] = packed
+        ncol_send[0, side] = packed.astype(BF16)
     key = owner[...] * (prows * pcols) + cell[...]
     keys[0] = jnp.broadcast_to(key, keys.shape[1:])
 
@@ -185,30 +185,68 @@
         high, low = split(x)
         return dot(lhs[...], jnp.concatenate([high, low, high], axis=0))
 
-    def beside(x, low, high, width):
+    def inside(x, width):
         lane = lax.broadcasted_iota(jnp.int32, (levels, width), 1)
-        before = jnp.where(lane == 0, low, pltpu.roll(x, 1, axis=1))
-        after = jnp.where(lane == width - 1, high, pltpu.roll(x, width - 1, axis=1))
+        before = jnp.where(lane == 0, 0.0, pltpu.roll(x, 1, axis=1))
+        after = jnp.where(lane == width - 1, 0.0, pltpu.roll(x, width - 1, axis=1))
         return before + after
 
+    def halo_matrix(scale):
+        high, low = split(vert_mix[...] * scale)
+        at = lax.broadcasted_iota(jnp.int32, (levels, 2 * levels), 0)
+        across = lax.broadcasted_iota(jnp.int32, (levels, 2 * levels), 1)
+        return (
+            dot(high, one_hot(across == at)) + dot(low, one_hot(across == at + levels))
+        ).astype(BF16)
+
+    parent_lhs = halo_matrix(nu_p[...])
+    nest_lhs = halo_matrix(nu_n[...] * (1.0 - relax[...]))
+
+    def from_halos(matrix, rows, cols):
+        halos = jnp.concatenate([rows[LOW], rows[HIGH], cols[LOW], cols[HIGH]], axis=1)
+        added = dot(matrix, jnp.concatenate([halos, halos], axis=0))
+        width = rows.shape[-1]
+        return (
+            added[:, :width], added[:, width:2 * width],
+            added[:, 2 * width:2 * width + 128], added[:, 2 * width + 128:],
+        )
+
+    def add_cols(target, r, width, low, high):
+        target[:, :128] = target[:, :128] + jnp.where(lane128 == 0, low[:, r:r + 1], 0.0)
+        target[:, width - 128:] = target[:, width - 128:] + jnp.where(
+            lane128 == 127, high[:, r:r + 1], 0.0)
+
+    for r in range(prows):
+        centre = parent[r].astype(F32)
+        around = inside(centre, pcols)
+        if r > 0:
+            around = around + parent[r - 1].astype(F32)
+        if r < prows - 1:
+            around = around + parent[r + 1].astype(F32)
+        stepped[r] = mix(centre + nu_parent_c * (around - 4.0 * centre))
     for side in (LOW, HIGH):
         parent_halo(side, "recv")
-    p_low, p_high = pcol[LOW].astype(F32), pcol[HIGH].astype(F32)
+    row_low, row_high, col_low, col_high = from_halos(parent_lhs, prow, pcol)
+    stepped[0] = stepped[0] + row_low
+    stepped[prows - 1] = stepped[prows - 1] + row_high
     for r in range(prows):
-        centre = parent[r].astype(F32)
-        above = (parent[r - 1] if r > 0 else prow[LOW]).astype(F32)
-        below = (parent[r + 1] if r < prows - 1 else prow[HIGH]).astype(F32)
-        around = above + below + beside(centre, p_low[:, r:r + 1], p_high[:, r:r + 1], pcols)
-        out = mix(centre + nu_parent_c * (around - 4.0 * centre))
-        stepped[r] = out
-        stepped_bf[r * levels:(r + 1) * levels, :] = out.astype(BF16)
+        add_cols(stepped.at[r], r, pcols, col_low, col_high)
+        stepped_bf[r * levels:(r + 1) * levels, :] = stepped[r].astype(BF16)
 
     parent_col = lax.broadcasted_iota(jnp.int32, (pcols, blocks), 0)
     shift = pcols.bit_length() - 1
 
+    def row_of(k):
+        return lax.shift_right_arithmetic(keys[k, 0:1, :] - me * (prows * pcols), shift)
+
     def places(k):
-        here = keys[k, 0:1, :] - me * (prows * pcols)
-        return lax.shift_right_arithmetic(here, shift), one_hot(parent_col == (here & (pcols - 1)))
+        return row_of(k), one_hot(parent_col == (keys[k, 0:1, :] & (pcols - 1)))
+
+    parent_across = lax.broadcasted_iota(jnp.int32, (blocks, pcols), 1)
+
+    def place_back(k):
+        down = jnp.transpose(keys[k])[:, 0:1]
+        back[k] = one_hot(parent_across == (down & (pcols - 1)))
 
     def serve(k):
         if not (isinstance(k, int) and k == 0):
@@ -234,33 +272,37 @@
 
     weights = [weight(me * nrows + r - 1) for r in range(nrows + 1)]
 
-    def diffuse(turn, get, put):
-        low, high = ncol[turn, LOW].astype(F32), ncol[turn, HIGH].astype(F32)
+    def diffuse(get, put):
         for r in range(nrows):
             centre = get(r)
-            above = get(r - 1) if r > 0 else nrow[turn, LOW].astype(F32)
-            below = get(r + 1) if r < nrows - 1 else nrow[turn, HIGH].astype(F32)
-            around = (
-                above * weights[r] + below * weights[r + 1]
-                + beside(centre, low[:, r:r + 1], high[:, r:r + 1], ncols)
-            )
+            around = inside(centre, ncols)
+            if r > 0:
+                around = around + get(r - 1) * weights[r]
+            if r < nrows - 1:
+                around = around + get(r + 1) * weights[r + 1]
             put(r, mix(keep_c * (centre + nu_nest_c * (around - 4.0 * centre))))
 
-    for side in (LOW, HIGH):
-        nest_halo(0, side, "recv")
+    def nest_halos(turn):
+        for side in (LOW, HIGH):
+            nest_halo(turn, side, "recv")
+        row_low, row_high, col_low, col_high = from_halos(nest_lhs, nrow.at[turn], ncol.at[turn])
+        return row_low * weights[0], row_high * weights[nrows], col_low, col_high
 
     def put_state(r, value):
         state[0, r] = value
 
-    diffuse(0, lambda r: nest[r].astype(F32), put_state)
+    diffuse(lambda r: nest[r].astype(F32), put_state)
+    row_low, row_high, col_low, col_high = nest_halos(0)
+    state[0, 0] = state[0, 0] + row_low
+    state[0, nrows - 1] = state[0, nrows - 1] + row_high
+    for r in range(nrows):
+        add_cols(state.at[0, r], r, ncols, col_low, col_high)
 
     parent_row = lax.broadcasted_iota(jnp.int32, (16, blocks), 0)
+    over(0, n_x, place_back)
 
     def count_step(k):
-        row, hot = places(k)
-        return lax.dot_general(
-            one_hot(parent_row == row), hot, (((1,), (1,)), ((), ())), preferred_element_type=F32
-        )
+        return dot(one_hot(parent_row == row_of(k)), back[k])
 
     forced = answers[0].astype(F32)
     if n_x <= 8:
@@ -290,63 +332,71 @@
         pulled[a] = dot(jnp.concatenate([high, low], axis=1), spread2)
 
     def send_rows(turn, r, value):
-        if r == 0:
-            nrow_send[turn - 1, LOW] = value.astype(BF16)
-            nest_halo(turn, LOW, "start", ("x",))
-        if r == nrows - 1:
-            nrow_send[turn - 1, HIGH] = value.astype(BF16)
-            nest_halo(turn, HIGH, "start", ("x",))
-
-    def send_cols(turn, slot):
-        rows = [state[slot, r] for r in range(nrows)]
-        for side, packed in enumerate(edges(rows, ncols)):
-            ncol_send[turn, side] = packed
-            nest_halo(turn, side, "start", ("y",))
+        side = LOW if r == 0 else HIGH
+        nrow_send[turn - 1, side] = value.astype(BF16)
+        nest_halo(turn, side, "start", ("x",))
 
     for r in (0, nrows - 1, *range(1, nrows - 1)):
         value = state[0, r] + pulled[r // 3]
         state[0, r] = value
-        send_rows(1, r, value)
-    send_cols(1, 0)
+        if r in (0, nrows - 1):
+            send_rows(1, r, value)
+    for side, packed in enumerate(edges([state[0, r] for r in range(nrows)], ncols)):
+        ncol_send[1, side] = packed.astype(BF16)
+        nest_halo(1, side, "start", ("y",))
 
     for turn in range(1, TURNS):
-        for side in (LOW, HIGH):
-            nest_halo(turn, side, "recv")
         now, later = (turn - 1) % 2, turn % 2
 
         def put_next(r, value):
-            value = value + pulled[r // 3]
-            state[later, r] = value
+            state[later, r] = value + pulled[r // 3]
+
+        diffuse(lambda r: state[now, r], put_next)
+        ends = None
+        if turn < TURNS - 1:
+            ends = edges([state[later, r] for r in range(nrows)], ncols)
+        row_low, row_high, col_low, col_high = nest_halos(turn)
+        for r, added in ((0, row_low), (nrows - 1, row_high)):
+            state[later, r] = state[later, r] + added
+            add_cols(state.at[later, r], r, ncols, col_low, col_high)
             if turn < TURNS - 1:
-                send_rows(turn + 1, r, value)
-            else:
-                nest_out[r] = value.astype(BF16)
-
-        diffuse(turn, lambda r: state[now, r], put_next)
+                send_rows(turn + 1, r, state[later, r])
         if turn < TURNS - 1:
-            send_cols(turn + 1, later)
+            for side, (end, at, own) in enumerate(
+                zip(ends, (0, ncols - 1), (col_low, col_high))
+            ):
+                end = end + own
+                end = end + jnp.where(lane128 == 0, row_low[:, at:at + 1], 0.0)
+                end = end + jnp.where(lane128 == nrows - 1, row_high[:, at:at + 1], 0.0)
+                ncol_send[turn + 1, side] = end.astype(BF16)
+                nest_halo(turn + 1, side, "start", ("y",))
+        for r in range(1, nrows - 1):
+            add_cols(state.at[later, r], r, ncols, col_low, col_high)
 
     last = (TURNS - 1) % 2
+    down_cell = lax.broadcasted_iota(jnp.int32, (ncols, bcols), 0)
+    down_block = lax.broadcasted_iota(jnp.int32, (ncols, bcols), 1)
+    gather_up = one_hot((down_cell >= 3 * down_block) & (down_cell < 3 * down_block + 3))
     for a in range(brows):
         summed = state[last, 3 * a] + state[last, 3 * a + 1] + state[last, 3 * a + 2]
         high, low = split(summed)
-        both = lax.dot_general(
-            jnp.concatenate([high, low], axis=0), spread,
-            (((1,), (1,)), ((), ())), preferred_element_type=F32,
-        )
+        both = dot(jnp.concatenate([high, low], axis=0), gather_up)
         mean = (both[:levels] + both[levels:]) * (1.0 / 9.0)
         means[0, :, a * bcols:(a + 1) * bcols] = mean.astype(BF16)
     over(1, n_x, lambda k: mean_copy(k).start())
+    for r in range(nrows):
+        nest_out[r] = state[last, r].astype(BF16)
 
     def give(k, total):
-        row, hot = places(k)
+        row = row_of(k)
         mean = means[k].astype(F32)
         shared = jnp.concatenate(
             [jnp.where(row == r, mean, 0.0).astype(BF16) for r in range(prows)], axis=0
         )
-        return total + lax.dot_general(
-            shared, hot, (((1,), (1,)), ((), ())), preferred_element_type=F32)
-
+        return total + dot(shared, back[k])
+
+    for r in range(prows):
+        stepped[r] = stepped[r] * (1.0 - feedback_c * counts[r:r + 1, :])
     returned = give(0, jnp.zeros((prows * levels, pcols), F32))
     if n_x <= 8:
         for k in range(1, n_x):
@@ -359,9 +409,8 @@
 
         returned = lax.fori_loop(1, n_x, give_next, returned)
     for r in range(prows):
-        own = stepped[r]
-        back = returned[r * levels:(r + 1) * levels] - counts[r:r + 1, :] * own
-        parent_out[r] = (own + feedback_c * back).astype(BF16)
+        given = returned[r * levels:(r + 1) * levels]
+        parent_out[r] = (stepped[r] + feedback_c * given).astype(BF16)
 
     for side in (LOW, HIGH):
         parent_halo(side, "send")
@@ -408,6 +457,7 @@
             pltpu.VMEM((n_x, levels, blocks), BF16),
             pltpu.VMEM((levels, 3 * levels), BF16),
             pltpu.VMEM((nrows // 3, levels, ncols), F32),
+            pltpu.VMEM((n_x, blocks, pcols), BF16),
             dma((1 + TURNS, 2)), dma((1 + TURNS, 2)), dma((1 + TURNS, 2)), dma((1 + TURNS, 2)),
             dma((n_x,)), dma((n_x,)), dma((n_x,)), dma((n_x,)), dma((n_x,)), dma((n_x,)),
         ],

time: 34.3 us -> 32.7 us (0.953)
  Pallas kernels: 30.1 us -> 28.5 us
    pallas_call x1, Pallas kernels: 30.1 us -> 28.5 us  [body(): pl.pallas_call(functools.partial(kernel, n_x, n_gy, n_gz), out_shape=(jax...]
where the time goes in v2:
time: 32.7 us; the launch traced here: 32.5 us
  Pallas kernels  28.5 us (87%)
  local copies, waits for them, and re-layouts  3.26 us (10%)
  between operations  0.77 us (2%)
    pallas_call x1, Pallas kernels, body(): pl.pallas_call(functools.partial(kernel, n_x, n_gy, n_gz), out_shape=(jax...  28.5 us
    unnamed x21, local copies, waits for them, and re-layouts  3.26 us

profile of v2, /device:TPU:0, one launch (start us, length us, event | category | flops | bytes accessed | tf_op | source)
XLA Modules:
  0.0 32.5 jit_solution(13798442248656191916)
XLA Ops:
  0.6 0.0 copy-start
  0.6 0.0 copy-start.1
  0.7 0.0 copy-start.3
  0.7 0.0 copy-start.5
  0.7 0.0 copy-start.6
  0.7 0.0 copy-start.7
  0.7 0.0 copy-start.8
  0.7 1.1 %copy.15 = bf16[80,8,256]{2,0,1:T(8,128)(2,1)S(1)} copy(bf16[80,8,256]{2,1,0:T(8,128)(2,1)} %param.10) | data formatting | bytes 655360 | tf_op args[0]
  1.8 0.0 copy-start.2
  1.8 0.0 copy-start.4
  1.8 0.0 copy-done
  1.8 0.0 copy-done.1
  1.8 0.0 copy-done.3
  1.8 0.0 copy-done.5
  1.8 0.0 copy-done.6
  1.9 0.0 copy-done.7
  1.9 0.0 copy-done.8
  1.9 0.6 %copy-done.2 = s32[1,1,256,1]{2,3,1,0:T(1,128)S(1)} copy-done((s32[1,1,256,1]{2,3,1,0:T(1,128)S(1)}, s32[1,1,256,1]{2,3,1,0:T(1,128)}, u32[]{:S(2)}) %copy-start.2) | copy-done | bytes 1048
  2.5 0.0 copy-done.4
  2.5 28.5 %shard_map.113 = (bf16[8,80,256]{2,1,0:T(8,128)(2,1)S(1)}, bf16[6,80,384]{2,1,0:T(8,128)(2,1)S(1)}) custom-call(bf16[8,80,256]{2,1,0:T(8,128)(2,1)S(1)} %bitcast.12, bf16[6,80,384]{2,1,0:T(8,128)(2,1)S(1)} %bitcast.13, f32[1,80]{1,0:T(1,128)S(1)} %bitcast.18, f32[1,80]{1,0:T(1,128)S(1)} %bitcast.19, f32[1,80]{1,0:T(1,128)S(1)} %bitcast.20, ...), custom_call_target="tpu_custom_call" | custom-call | tf_op jit(solution)/shard_map/pallas_call | solution.py:435
  31.0 0.8 %copy.13 = bf16[80,8,256]{2,1,0:T(8,128)(2,1)} copy(bf16[80,8,256]{2,0,1:T(8,128)(2,1)S(1)} %bitcast.15) | data formatting | bytes 655360
  31.8 0.7 %copy.17 = bf16[80,6,384]{2,0,1:T(8,128)(2,1)} copy(bf16[80,6,384]{2,0,1:T(8,128)(2,1)S(1)} %bitcast.14) | data formatting | bytes 737280
Async XLA Ops:
  0.6 1.2 %copy-start = (bf16[80,6,384]{2,0,1:T(8,128)(2,1)S(1)}, bf16[80,6,384]{2,0,1:T(8,128)(2,1)}, u32[]{:S(2)}) copy-start(bf16[80,6,384]{2,0,1:T(8,128)(2,1)} %param.11) | copy-start | bytes 1105924
  0.6 1.2 %copy-start.1 = (f32[80,80]{1,0:T(8,128)S(1)}, f32[80,80]{1,0:T(8,128)}, u32[]{:S(2)}) copy-start(f32[80,80]{1,0:T(8,128)} %vert_mix.1) | copy-start | bytes 76804
  0.7 1.2 %copy-start.3 = (s32[1,1,256]{2,1,0:T(1,128)S(1)}, s32[1,1,256]{2,1,0:T(1,128)}, u32[]{:S(2)}) copy-start(s32[1,1,256]{2,1,0:T(1,128)} %param.18) | copy-start | bytes 3076
  0.7 1.2 %copy-start.5 = (f32[80]{0:T(128)S(1)}, f32[80]{0:T(128)}, u32[]{:S(2)}) copy-start(f32[80]{0:T(128)} %param.13) | copy-start | bytes 964
  0.7 1.2 %copy-start.6 = (f32[80]{0:T(128)S(1)}, f32[80]{0:T(128)}, u32[]{:S(2)}) copy-start(f32[80]{0:T(128)} %param.14) | copy-start | bytes 964
  0.7 1.2 %copy-start.7 = (f32[80]{0:T(128)S(1)}, f32[80]{0:T(128)}, u32[]{:S(2)}) copy-start(f32[80]{0:T(128)} %param.15) | copy-start | bytes 964
  0.7 1.2 %copy-start.8 = (s32[24]{0:T(128)S(1)}, s32[24]{0:T(128)}, u32[]{:S(2)}) copy-start(s32[24]{0:T(128)} %nest_of.1) | copy-start | bytes 292
  1.8 0.7 %copy-start.2 = (s32[1,1,256,1]{2,3,1,0:T(1,128)S(1)}, s32[1,1,256,1]{2,3,1,0:T(1,128)}, u32[]{:S(2)}) copy-start(s32[1,1,256,1]{2,3,1,0:T(1,128)} %param.17) | copy-start | bytes 3076
  1.8 0.7 %copy-start.4 = (f32[80]{0:T(128)S(1)}, f32[80]{0:T(128)}, u32[]{:S(2)}) copy-start(f32[80]{0:T(128)} %param.12) | copy-start | bytes 964

commit v3 on v2

--- a/solution.py
+++ b/solution.py
@@ -37,12 +37,24 @@
 
 def kernel(
     n_x, n_gy, n_gz,
-    parent, nest, nu_p, nu_n, relax, feedback, vert_mix, owner, cell, nest_of,
-    parent_out, nest_out,
+    parent_h, nest_h, nu_p_h, nu_n_h, relax_h, feedback_h, vert_mix_h, owner_h, cell_h, nest_of_h,
+    parent_out, nest_out_h,
+    parent_n, nest, nu_p, nu_n, relax, feedback, vert_mix, owner, cell, nest_of, turned, parent,
+    in_sem, nest_out, out_sem,
     keys, prow, pcol, pcol_send, nrow, nrow_send, ncol, ncol_send,
     state, stepped, stepped_bf, answers, answers_send, means, lhs, pulled, back,
     row_s, row_r, col_s, col_r, key_s, key_r, ans_s, ans_r, mean_s, mean_r,
 ):
+    loads = [
+        pltpu.make_async_copy(src, dst, in_sem.at[i])
+        for i, (src, dst) in enumerate((
+            (parent_h, parent_n), (nest_h, nest), (owner_h, owner), (cell_h, cell),
+            (vert_mix_h, vert_mix), (nu_p_h, nu_p), (nu_n_h, nu_n), (relax_h, relax),
+            (feedback_h, feedback), (nest_of_h, nest_of),
+        ))
+    ]
+    for load in loads:
+        load.start()
     prows, levels, pcols = parent.shape
     nrows, _, ncols = nest.shape
     brows, bcols = nrows // 3, ncols // 3
@@ -84,7 +96,18 @@
         high = pack([rows[r][:, width - 1:width] for r in range(len(rows))])
         return low, high
 
-    p = [parent[r].astype(F32) for r in range(prows)]
+    for load in loads:
+        load.wait()
+    whole = parent_n[...].astype(F32)
+    p = []
+    for h in range(pcols // 128):
+        turned[h] = whole[:, :, h * 128:(h + 1) * 128].reshape(levels * prows, 128)
+    for r in range(prows):
+        row = jnp.concatenate(
+            [turned[h, pl.ds(r, levels, stride=prows), :] for h in range(pcols // 128)], axis=1
+        )
+        parent[r] = row.astype(BF16)
+        p.append(row)
     for side, packed in enumerate(edges(p, pcols)):
         pcol_send[side] = packed.astype(BF16)
     s = [nest[r].astype(F32) for r in range(nrows)]
@@ -105,6 +128,57 @@
             pcol[side] = jnp.zeros(pcol.shape[1:], BF16)
             for turn in range(TURNS):
                 ncol[turn, side] = jnp.zeros(ncol.shape[2:], BF16)
+
+    def level_column(ref):
+        at = lax.broadcasted_iota(jnp.int32, (levels, levels), 0)
+        across = lax.broadcasted_iota(jnp.int32, (levels, levels), 1)
+        return jnp.sum(jnp.where(at == across, ref[...], 0.0), axis=1, keepdims=True)
+
+    nu_parent_c, nu_nest_c = level_column(nu_p), level_column(nu_n)
+    relax_c, feedback_c = level_column(relax), level_column(feedback)
+    keep_c = 1.0 - relax_c
+
+    m_high, m_low = split(vert_mix[...])
+    wide_at = lax.broadcasted_iota(jnp.int32, (levels, 3 * levels), 0)
+    wide_across = lax.broadcasted_iota(jnp.int32, (levels, 3 * levels), 1)
+    place_high = one_hot((wide_across == wide_at) | (wide_across == wide_at + levels))
+    place_low = one_hot(wide_across == wide_at + 2 * levels)
+    lhs[...] = (dot(m_high, place_high) + dot(m_low, place_low)).astype(BF16)
+
+    def mix(x):
+        high, low = split(x)
+        return dot(lhs[...], jnp.concatenate([high, low, high], axis=0))
+
+    def inside(x, width):
+        lane = lax.broadcasted_iota(jnp.int32, (levels, width), 1)
+        before = jnp.where(lane == 0, 0.0, pltpu.roll(x, 1, axis=1))
+        after = jnp.where(lane == width - 1, 0.0, pltpu.roll(x, width - 1, axis=1))
+        return before + after
+
+    def halo_matrix(scale):
+        high, low = split(vert_mix[...] * scale)
+        at = lax.broadcasted_iota(jnp.int32, (levels, 2 * levels), 0)
+        across = lax.broadcasted_iota(jnp.int32, (levels, 2 * levels), 1)
+        return (
+            dot(high, one_hot(across == at)) + dot(low, one_hot(across == at + levels))
+        ).astype(BF16)
+
+    parent_lhs = halo_matrix(nu_p[...])
+    nest_lhs = halo_matrix(nu_n[...] * (1.0 - relax[...]))
+
+    def from_halos(matrix, rows, cols):
+        halos = jnp.concatenate([rows[LOW], rows[HIGH], cols[LOW], cols[HIGH]], axis=1)
+        added = dot(matrix, jnp.concatenate([halos, halos], axis=0))
+        width = rows.shape[-1]
+        return (
+            added[:, :width], added[:, width:2 * width],
+            added[:, 2 * width:2 * width + 128], added[:, 2 * width + 128:],
+        )
+
+    def add_cols(target, r, width, low, high):
+        target[:, :128] = target[:, :128] + jnp.where(lane128 == 0, low[:, r:r + 1], 0.0)
+        target[:, width - 128:] = target[:, width - 128:] + jnp.where(
+            lane128 == 127, high[:, r:r + 1], 0.0)
 
     callers = n_x - 1 + sum(present.astype(jnp.int32) for present, _ in y_side)
     pl.semaphore_wait(barrier, callers)
@@ -164,57 +238,6 @@
     over(1, n_x, lambda k: key_copy(k).start())
     for side in (LOW, HIGH):
         nest_halo(0, side, "start")
-
-    def level_column(ref):
-        at = lax.broadcasted_iota(jnp.int32, (levels, levels), 0)
-        across = lax.broadcasted_iota(jnp.int32, (levels, levels), 1)
-        return jnp.sum(jnp.where(at == across, ref[...], 0.0), axis=1, keepdims=True)
-
-    nu_parent_c, nu_nest_c = level_column(nu_p), level_column(nu_n)
-    relax_c, feedback_c = level_column(relax), level_column(feedback)
-    keep_c = 1.0 - relax_c
-
-    m_high, m_low = split(vert_mix[...])
-    wide_at = lax.broadcasted_iota(jnp.int32, (levels, 3 * levels), 0)
-    wide_across = lax.broadcasted_iota(jnp.int32, (levels, 3 * levels), 1)
-    place_high = one_hot((wide_across == wide_at) | (wide_across == wide_at + levels))
-    place_low = one_hot(wide_across == wide_at + 2 * levels)
-    lhs[...] = (dot(m_high, place_high) + dot(m_low, place_low)).astype(BF16)
-
-    def mix(x):
-        high, low = split(x)
-        return dot(lhs[...], jnp.concatenate([high, low, high], axis=0))
-
-    def inside(x, width):
-        lane = lax.broadcasted_iota(jnp.int32, (levels, width), 1)
-        before = jnp.where(lane == 0, 0.0, pltpu.roll(x, 1, axis=1))
-        after = jnp.where(lane == width - 1, 0.0, pltpu.roll(x, width - 1, axis=1))
-        return before + after
-
-    def halo_matrix(scale):
-        high, low = split(vert_mix[...] * scale)
-        at = lax.broadcasted_iota(jnp.int32, (levels, 2 * levels), 0)
-        across = lax.broadcasted_iota(jnp.int32, (levels, 2 * levels), 1)
-        return (
-            dot(high, one_hot(across == at)) + dot(low, one_hot(across == at + levels))
-        ).astype(BF16)
-
-    parent_lhs = halo_matrix(nu_p[...])
-    nest_lhs = halo_matrix(nu_n[...] * (1.0 - relax[...]))
-
-    def from_halos(matrix, rows, cols):
-        halos = jnp.concatenate([rows[LOW], rows[HIGH], cols[LOW], cols[HIGH]], axis=1)
-        added = dot(matrix, jnp.concatenate([halos, halos], axis=0))
-        width = rows.shape[-1]
-        return (
-            added[:, :width], added[:, width:2 * width],
-            added[:, 2 * width:2 * width + 128], added[:, 2 * width + 128:],
-        )
-
-    def add_cols(target, r, width, low, high):
-        target[:, :128] = target[:, :128] + jnp.where(lane128 == 0, low[:, r:r + 1], 0.0)
-        target[:, width - 128:] = target[:, width - 128:] + jnp.where(
-            lane128 == 127, high[:, r:r + 1], 0.0)
 
     for r in range(prows):
         centre = parent[r].astype(F32)
@@ -386,6 +409,8 @@
     over(1, n_x, lambda k: mean_copy(k).start())
     for r in range(nrows):
         nest_out[r] = state[last, r].astype(BF16)
+    store_nest = pltpu.make_async_copy(nest_out, nest_out_h, out_sem)
+    store_nest.start()
 
     def give(k, total):
         row = row_of(k)
@@ -423,6 +448,7 @@
         mean_copy(k).wait_send()
 
     over(1, n_x, sent)
+    store_nest.wait()
 
 
 def body(n_x, n_gy, n_gz, parent, nest, nu_p, nu_n, relax, feedback, vert_mix, owner, cell, nest_of):
@@ -430,7 +456,6 @@
     _, nrows, ncols = nest.shape
     blocks = cell.size
     vmem = pl.BlockSpec(memory_space=pltpu.VMEM)
-    smem = pl.BlockSpec(memory_space=pltpu.SMEM)
     dma = pltpu.SemaphoreType.DMA
     parent_out, nest_out = pl.pallas_call(
         functools.partial(kernel, n_x, n_gy, n_gz),
@@ -438,9 +463,20 @@
             jax.ShapeDtypeStruct((prows, levels, pcols), BF16),
             jax.ShapeDtypeStruct((nrows, levels, ncols), BF16),
         ),
-        in_specs=[vmem] * 9 + [smem],
-        out_specs=(vmem, vmem),
+        in_specs=[pl.BlockSpec(memory_space=pltpu.HBM)] * 10,
+        out_specs=(vmem, pl.BlockSpec(memory_space=pltpu.HBM)),
         scratch_shapes=[
+            pltpu.VMEM(parent.shape, BF16),
+            pltpu.VMEM((nrows, levels, ncols), BF16),
+            *[pltpu.VMEM((1, levels), F32)] * 4,
+            pltpu.VMEM((levels, levels), F32),
+            *[pltpu.VMEM((1, blocks), jnp.int32)] * 2,
+            pltpu.SMEM(nest_of.shape, jnp.int32),
+            pltpu.VMEM((pcols // 128, levels * prows, 128), F32),
+            pltpu.VMEM((prows, levels, pcols), BF16),
+            dma((10,)),
+            pltpu.VMEM((nrows, levels, ncols), BF16),
+            dma,
             pltpu.VMEM((n_x, 8, blocks), jnp.int32),
             pltpu.VMEM((2, levels, pcols), BF16),
             pltpu.VMEM((2, levels, 128), BF16),
@@ -462,10 +498,10 @@
             dma((n_x,)), dma((n_x,)), dma((n_x,)), dma((n_x,)), dma((n_x,)), dma((n_x,)),
         ],
         compiler_params=pltpu.CompilerParams(
-            collective_id=0, has_side_effects=True, vmem_limit_bytes=40 * 1024 * 1024
+            collective_id=0, has_side_effects=True, vmem_limit_bytes=62 * 1024 * 1024
         ),
     )(
-        parent.transpose(1, 0, 2), nest.transpose(1, 0, 2),
+        parent, nest.transpose(1, 0, 2),
         nu_p.reshape(1, -1), nu_n.reshape(1, -1), relax.reshape(1, -1), feedback.reshape(1, -1),
         vert_mix, owner.reshape(1, -1), cell.reshape(1, -1), nest_of,
     )

time: 32.7 us -> 32.1 us (0.982)
  local copies, waits for them, and re-layouts: 3.26 us -> 2.59 us
    unnamed x21 -> x4, local copies, waits for them, and re-layouts: 3.26 us -> 2.59 us
where the time goes in v3:
time: 32.1 us; the launch traced here: 31.9 us
  Pallas kernels  28.7 us (89%)
  local copies, waits for them, and re-layouts  2.59 us (8%)
  between operations  0.65 us (2%)
    pallas_call x1, Pallas kernels, body(): pl.pallas_call(functools.partial(kernel, n_x, n_gy, n_gz), out_shape=(jax...  28.7 us
    unnamed x4, local copies, waits for them, and re-layouts  2.59 us

profile of v3, /device:TPU:0, one launch (start us, length us, event | category | flops | bytes accessed | tf_op | source)
XLA Modules:
  0.0 31.9 jit_solution(18302431311141223018)
XLA Ops:
  0.6 28.7 %shard_map.113 = (bf16[8,80,256]{2,1,0:T(8,128)(2,1)}, bf16[6,80,384]{2,1,0:T(8,128)(2,1)}) custom-call(bf16[80,8,256]{2,1,0:T(8,128)(2,1)} %parent_h.1, bf16[6,80,384]{2,1,0:T(8,128)(2,1)} %bitcast.9, f32[1,80]{1,0:T(1,128)} %bitcast.14, f32[1,80]{1,0:T(1,128)} %bitcast.15, f32[1,80]{1,0:T(1,128)} %bitcast.16, f32[1,80]{1,0:T(1,128)} %bitcast.17, ...), custom_call_target="tpu_custom_call" | custom-call | tf_op jit(solution)/shard_map/pallas_call | solution.py:460
  29.3 0.0 copy-start
  29.3 1.8 %copy.12 = bf16[80,8,256]{2,1,0:T(8,128)(2,1)} copy(bf16[80,8,256]{2,0,1:T(8,128)(2,1)} %bitcast.11) | data formatting | bytes 655360
  31.2 0.0 copy-done
  31.2 0.7 %copy.14 = bf16[80,6,384]{2,0,1:T(8,128)(2,1)} copy(bf16[80,6,384]{2,0,1:T(8,128)(2,1)S(1)} %bitcast.10) | data formatting | bytes 737280
Async XLA Ops:
  29.3 1.9 %copy-start = (bf16[6,80,384]{2,1,0:T(8,128)(2,1)S(1)}, bf16[6,80,384]{2,1,0:T(8,128)(2,1)}, u32[]{:S(2)}) copy-start(bf16[6,80,384]{2,1,0:T(8,128)(2,1)} %get-tuple-element.5) | copy-start | bytes 1105924

commit v4 on v3

--- a/solution.py
+++ b/solution.py
@@ -435,7 +435,12 @@
         returned = lax.fori_loop(1, n_x, give_next, returned)
     for r in range(prows):
         given = returned[r * levels:(r + 1) * levels]
-        parent_out[r] = (stepped[r] + feedback_c * given).astype(BF16)
+        whole_row = stepped[r] + feedback_c * given
+        for h in range(pcols // 128):
+            turned[h, pl.ds(r, levels, stride=prows), :] = whole_row[:, h * 128:(h + 1) * 128]
+    for h in range(pcols // 128):
+        parent_out[:, :, h * 128:(h + 1) * 128] = turned[h].reshape(
+            levels, prows, 128).astype(BF16)
 
     for side in (LOW, HIGH):
         parent_halo(side, "send")
@@ -449,6 +454,15 @@
 
     over(1, n_x, sent)
     store_nest.wait()
+
+
+def hand_over(parent, nest, parent_out, nest_out, parent_sem, nest_sem):
+    first = pltpu.make_async_copy(parent, parent_out, parent_sem)
+    second = pltpu.make_async_copy(nest, nest_out, nest_sem)
+    first.start()
+    second.start()
+    first.wait()
+    second.wait()
 
 
 def body(n_x, n_gy, n_gz, parent, nest, nu_p, nu_n, relax, feedback, vert_mix, owner, cell, nest_of):
@@ -460,7 +474,7 @@
     parent_out, nest_out = pl.pallas_call(
         functools.partial(kernel, n_x, n_gy, n_gz),
         out_shape=(
-            jax.ShapeDtypeStruct((prows, levels, pcols), BF16),
+            jax.ShapeDtypeStruct((levels, prows, pcols), BF16),
             jax.ShapeDtypeStruct((nrows, levels, ncols), BF16),
         ),
         in_specs=[pl.BlockSpec(memory_space=pltpu.HBM)] * 10,
@@ -505,7 +519,19 @@
         nu_p.reshape(1, -1), nu_n.reshape(1, -1), relax.reshape(1, -1), feedback.reshape(1, -1),
         vert_mix, owner.reshape(1, -1), cell.reshape(1, -1), nest_of,
     )
-    return parent_out.transpose(1, 0, 2), nest_out.transpose(1, 0, 2)
+    hbm = pl.BlockSpec(memory_space=pltpu.HBM)
+    parent_out, nest_out = pl.pallas_call(
+        hand_over,
+        out_shape=(
+            jax.ShapeDtypeStruct(parent_out.shape, BF16),
+            jax.ShapeDtypeStruct(nest_out.shape, BF16),
+        ),
+        in_specs=[hbm, hbm],
+        out_specs=(hbm, hbm),
+        scratch_shapes=[dma, dma],
+        compiler_params=pltpu.CompilerParams(vmem_limit_bytes=62 * 1024 * 1024),
+    )(parent_out, nest_out)
+    return parent_out, nest_out.transpose(1, 0, 2)
 
 
 def solution(mesh):

time: 32.1 us -> 51.8 us (1.61)
  Pallas kernels: 28.7 us -> 51 us
  local copies, waits for them, and re-layouts: 2.59 us -> 0 us
    pallas_call x0 -> x1, Pallas kernels: none -> 22.2 us  [body(): pl.pallas_call(hand_over, out_shape=(jax.ShapeDtypeStruct(parent_out.shap...]
    unnamed x4 -> x0, local copies, waits for them, and re-layouts: 2.59 us -> none
where the time goes in v4:
time: 51.8 us; the launch traced here: 51.6 us
  Pallas kernels  51 us (98%)
  between operations  0.64 us (1%)
    pallas_call x1, Pallas kernels, body(): pl.pallas_call(functools.partial(kernel, n_x, n_gy, n_gz), out_shape=(jax...  28.8 us
    pallas_call x1, Pallas kernels, body(): pl.pallas_call(hand_over, out_shape=(jax.ShapeDtypeStruct(parent_out.shap...  22.2 us

profile of v4, /device:TPU:0, one launch (start us, length us, event | category | flops | bytes accessed | tf_op | source)
XLA Modules:
  0.0 51.6 jit_solution(16192723968798263851)
XLA Ops:
  0.6 28.8 %shard_map.113 = (bf16[80,8,256]{2,1,0:T(8,128)(2,1)}, bf16[6,80,384]{2,1,0:T(8,128)(2,1)}) custom-call(bf16[80,8,256]{2,1,0:T(8,128)(2,1)} %parent_h.1, bf16[6,80,384]{2,1,0:T(8,128)(2,1)} %bitcast.8, f32[1,80]{1,0:T(1,128)} %bitcast.11, f32[1,80]{1,0:T(1,128)} %bitcast.12, f32[1,80]{1,0:T(1,128)} %bitcast.13, f32[1,80]{1,0:T(1,128)} %bitcast.14, ...), custom_call_target="tpu_custom_call" | custom-call | tf_op jit(solution)/shard_map/pallas_call | solution.py:474
  29.4 22.2 %shard_map.114 = (bf16[80,8,256]{2,1,0:T(8,128)(2,1)}, bf16[6,80,384]{2,1,0:T(8,128)(2,1)}) custom-call(bf16[80,8,256]{2,1,0:T(8,128)(2,1)} %get-tuple-element.6.parent, bf16[6,80,384]{2,1,0:T(8,128)(2,1)} %get-tuple-element.7.nest), custom_call_target="tpu_custom_call" | custom-call | tf_op jit(solution)/shard_map/pallas_call | solution.py:523

commit v5 on v4

--- a/solution.py
+++ b/solution.py
@@ -456,13 +456,26 @@
     store_nest.wait()
 
 
-def hand_over(parent, nest, parent_out, nest_out, parent_sem, nest_sem):
-    first = pltpu.make_async_copy(parent, parent_out, parent_sem)
-    second = pltpu.make_async_copy(nest, nest_out, nest_sem)
-    first.start()
-    second.start()
-    first.wait()
-    second.wait()
+def hand_over(parent, nest, parent_out, nest_out, parent_held, nest_held, in_sem, out_sem):
+    coming, going = [], []
+    for source, held, target in (
+        (parent, parent_held, parent_out), (nest, nest_held, nest_out)
+    ):
+        half = source.shape[0] // 2
+        for first in (0, half):
+            part = pl.ds(first, half)
+            i = len(coming)
+            coming.append(
+                pltpu.make_async_copy(source.at[part], held.at[part], in_sem.at[i]))
+            going.append(
+                pltpu.make_async_copy(held.at[part], target.at[part], out_sem.at[i]))
+    for come in coming:
+        come.start()
+    for come, go in zip(coming, going):
+        come.wait()
+        go.start()
+    for go in going:
+        go.wait()
 
 
 def body(n_x, n_gy, n_gz, parent, nest, nu_p, nu_n, relax, feedback, vert_mix, owner, cell, nest_of):
@@ -528,7 +541,10 @@
         ),
         in_specs=[hbm, hbm],
         out_specs=(hbm, hbm),
-        scratch_shapes=[dma, dma],
+        scratch_shapes=[
+            pltpu.VMEM(parent_out.shape, BF16), pltpu.VMEM(nest_out.shape, BF16),
+            dma((4,)), dma((4,)),
+        ],
         compiler_params=pltpu.CompilerParams(vmem_limit_bytes=62 * 1024 * 1024),
     )(parent_out, nest_out)
     return parent_out, nest_out.transpose(1, 0, 2)

time: 51.8 us -> 31.5 us (0.61)
  Pallas kernels: 51 us -> 30.7 us
    pallas_call x1, Pallas kernels: 22.2 us -> 1.91 us  [body(): pl.pallas_call(hand_over, out_shape=(jax.ShapeDtypeStruct(parent_out.shap...]
where the time goes in v5:
time: 31.5 us; the launch traced here: 31.3 us
  Pallas kernels  30.7 us (97%)
  between operations  0.64 us (2%)
    pallas_call x1, Pallas kernels, body(): pl.pallas_call(functools.partial(kernel, n_x, n_gy, n_gz), out_shape=(jax...  28.8 us
    pallas_call x1, Pallas kernels, body(): pl.pallas_call(hand_over, out_shape=(jax.ShapeDtypeStruct(parent_out.shap...  1.91 us

profile of v5, /device:TPU:0, one launch (start us, length us, event | category | flops | bytes accessed | tf_op | source)
XLA Modules:
  0.0 31.3 jit_solution(2901368481424514446)
XLA Ops:
  0.6 28.8 %shard_map.113 = (bf16[80,8,256]{2,1,0:T(8,128)(2,1)}, bf16[6,80,384]{2,1,0:T(8,128)(2,1)}) custom-call(bf16[80,8,256]{2,1,0:T(8,128)(2,1)} %parent_h.1, bf16[6,80,384]{2,1,0:T(8,128)(2,1)} %bitcast.8, f32[1,80]{1,0:T(1,128)} %bitcast.11, f32[1,80]{1,0:T(1,128)} %bitcast.12, f32[1,80]{1,0:T(1,128)} %bitcast.13, f32[1,80]{1,0:T(1,128)} %bitcast.14, ...), custom_call_target="tpu_custom_call" | custom-call | tf_op jit(solution)/shard_map/pallas_call | solution.py:487
  29.4 1.9 %shard_map.114 = (bf16[80,8,256]{2,1,0:T(8,128)(2,1)}, bf16[6,80,384]{2,1,0:T(8,128)(2,1)}) custom-call(bf16[80,8,256]{2,1,0:T(8,128)(2,1)} %get-tuple-element.6.parent, bf16[6,80,384]{2,1,0:T(8,128)(2,1)} %get-tuple-element.7.nest), custom_call_target="tpu_custom_call" | custom-call | tf_op jit(solution)/shard_map/pallas_call | solution.py:536
